TPU v7x, 256 devices: a whole 4x4x8 slice. The times are simulated.
256 devices in a mesh: leaf: 64 (over x, z, core), rhs: 4 (over y).
Axes of the slice: x: 4, y: 4, z: 8, core: 2. Of those that a mesh axis runs over, the one named last changes fastest.
Arguments:
- points: float32 [8, 262144], P(None, 'leaf'), may hold values from -6 to 6
- charges: bfloat16 [262144, 512], P('leaf', 'rhs'), may hold values from -6 to 6
- tree_order: int32 [262144], P('leaf'), may hold values from 0 to 262143, as said below
- leaf_basis: bfloat16 [1024, 256, 128], P('leaf'), may hold values from -0.375 to 0.375
- local_transfer: bfloat16 [1984, 128, 128], P('leaf'), may hold values from -0.4375 to 0.4375
- local_coupling: bfloat16 [960, 128, 128], P('leaf'), may hold values from -0.5 to 0.5
- top_transfer: bfloat16 [62, 128, 128], replicated, may hold values from -0.4375 to 0.4375
- top_coupling: bfloat16 [63, 128, 128], replicated, may hold values from -0.5 to 0.5
Outputs:
- potential: float32 [262144, 512], P('leaf', 'rhs')
Inputs may be any that keep to these rules, and one draw needn't show every extreme that they name: `tree_order`: each block of 256 consecutive positions (one leaf) holds each point of that same block exactly once.
All inputs are finite; a program needn't handle non-finite values.
Results may differ from a plain program's by a relative error of at most 0.0025.
Values may be sent and summed in bfloat16 or wider, within the bound.
A program may use at most 128 MiB of HBM per device.

v0:
```python
import jax
import jax.numpy as jnp
from jax import lax
from jax.sharding import PartitionSpec as P

KERNEL_RATE = 0.1
RIDGE_SHIFT = 0.5


def swapped(block, axis, stride):
    count = lax.axis_size(axis)
    route = []
    for low in range(count):
        high = low | 1 << stride
        if high != low and high < count:
            route += [(low, high), (high, low)]
    return lax.ppermute(block, axis, route)


def kernel_blocks(coords):
    width = coords.shape[2]
    total = jnp.zeros((coords.shape[0], width, width), jnp.float32)
    for column in range(coords.shape[1]):
        spread = coords[:, column, :, None] - coords[:, column, None, :]
        total = total + spread * spread
    blocks = jnp.exp(-KERNEL_RATE * total) + RIDGE_SHIFT * jnp.eye(width, dtype=jnp.float32)
    return blocks.astype(jnp.bfloat16)


def leaf_terms(coords, values, basis):
    blocks = kernel_blocks(coords)
    direct = jnp.einsum("lpq,lqc->lpc", blocks, values, preferred_element_type=jnp.float32)
    upward = jnp.einsum("lpr,lpc->lrc", basis, values, preferred_element_type=jnp.float32)
    return (direct, upward)


def apply_batch(mats, vectors, transposed):
    high = lax.Precision.HIGHEST
    if transposed:
        return jnp.einsum("nrs,nrc->nsc", mats.astype(jnp.float32), vectors, precision=high)
    return jnp.einsum("nrs,nsc->nrc", mats.astype(jnp.float32), vectors, precision=high)


def apply_single(matrix, vector):
    return jnp.dot(matrix.astype(jnp.float32), vector, precision=lax.Precision.HIGHEST)


def couple_pairs(mats, nodes):
    high = lax.Precision.HIGHEST
    wide = mats.astype(jnp.float32)
    to_left = jnp.einsum("nrs,nsc->nrc", wide, nodes[1::2], precision=high)
    to_right = jnp.einsum("nsr,nsc->nrc", wide, nodes[0::2], precision=high)
    return jnp.stack((to_left, to_right), axis=1).reshape(nodes.shape)


def local(
    points,
    charges,
    tree_order,
    leaf_basis,
    local_transfer,
    local_coupling,
    top_transfer,
    top_coupling,
):
    high = lax.Precision.HIGHEST
    leaf_count = leaf_basis.shape[0]
    width = leaf_basis.shape[1]
    rank = leaf_basis.shape[2]
    rows = charges.shape[0]
    columns = charges.shape[1]
    devices = lax.axis_size("leaf")
    groups = lax.axis_size("rhs")
    mine = lax.axis_index("leaf")
    leaf_starts = mine * rows + jnp.arange(leaf_count, dtype=jnp.int32)[:, None] * width
    positions = tree_order.reshape(leaf_count, width) - leaf_starts
    slots = jnp.arange(width, dtype=jnp.int32)
    picker = positions[:, :, None] == slots[None, None, :]
    picker_wide = picker.astype(jnp.float32)
    ordered = jnp.einsum(
        "lpq,lqc->lpc",
        picker.astype(jnp.bfloat16),
        charges.reshape(leaf_count, width, columns),
        preferred_element_type=jnp.float32,
    ).astype(jnp.bfloat16)
    stored = points.reshape(points.shape[0], leaf_count, width)
    coords = jnp.einsum("dlq,lpq->ldp", stored, picker_wide, precision=high)
    quarter = leaf_count // groups
    spread_cols = lax.all_to_all(ordered, "rhs", split_axis=0, concat_axis=2, tiled=True)
    first = lax.axis_index("rhs") * quarter
    own_coords = lax.dynamic_slice_in_dim(coords, first, quarter, 0)
    own_basis = lax.dynamic_slice_in_dim(leaf_basis, first, quarter, 0)
    direct_part, upward_part = leaf_terms(own_coords, spread_cols, own_basis)
    direct, upward = (
        lax.all_to_all(direct_part, "rhs", split_axis=2, concat_axis=0, tiled=True),
        lax.all_to_all(upward_part, "rhs", split_axis=2, concat_axis=0, tiled=True),
    )
    levels_low = leaf_count.bit_length() - 1
    ups = [upward]
    offset = 0
    for height in range(levels_low):
        count = leaf_count >> height
        projected = apply_batch(local_transfer[offset : offset + count], ups[-1], True)
        ups.append(projected.reshape(count // 2, 2, rank, columns).sum(axis=1))
        offset = offset + count
    root_matrix = local_transfer[offset]
    sides = []
    pair_offset = 0
    for height in range(levels_low):
        count = leaf_count >> height + 1
        sides.append(couple_pairs(local_coupling[pair_offset : pair_offset + count], ups[height]))
        pair_offset = pair_offset + count
    levels_top = devices.bit_length() - 1

    def transfer_above(height):
        index = devices - (devices >> height - 1) + (mine >> height)
        return lax.dynamic_index_in_dim(top_transfer, index, 0, keepdims=False)

    current = ups[-1][0]
    projected = apply_single(root_matrix.T, current)
    tops = []
    for height in range(levels_top):
        other_now, other_proj = swapped((current, projected), "leaf", height)
        coupling_index = devices - (devices >> height) + (mine >> height + 1)
        coupling_matrix = lax.dynamic_index_in_dim(top_coupling, coupling_index, 0, keepdims=False)
        left_side = (mine >> height) % 2 == 0
        tops.append(
            apply_single(jnp.where(left_side, coupling_matrix, coupling_matrix.T), other_now)
        )
        current = projected + other_proj
        if height + 1 < levels_top:
            projected = apply_single(transfer_above(height + 1).T, current)
    above = jnp.zeros((rank, columns), jnp.float32)
    for height in reversed(range(levels_top)):
        matrix = root_matrix if height == 0 else transfer_above(height)
        above = tops[height] + apply_single(matrix, above)
    downs = above[None]
    for height in reversed(range(levels_low)):
        count = leaf_count >> height
        start = 2 * leaf_count - 2 * count
        downs = sides[height] + apply_batch(
            local_transfer[start : start + count], jnp.repeat(downs, 2, axis=0), False
        )
    final = direct + jnp.einsum(
        "lpr,lrc->lpc", leaf_basis.astype(jnp.float32), downs, precision=high
    )
    placed = jnp.einsum("lpq,lpc->lqc", picker_wide, final, precision=high)
    return placed.reshape(rows, columns)


def solution(mesh):
    placed = (
        P(None, "leaf"),
        P("leaf", "rhs"),
        P("leaf"),
        P("leaf", None, None),
        P("leaf", None, None),
        P("leaf", None, None),
        P(),
        P(),
    )
    return jax.shard_map(
        local, mesh=mesh, in_specs=placed, out_specs=P("leaf", "rhs"), check_vma=False
    )
```

profile of v0, /device:TPU:8, one launch (start us, length us, event | category | flops | bytes accessed | tf_op | source)
XLA Modules:
  0.0 126.1 jit_solution(5478529601729485665)
XLA Ops:
  1.0 3.5 %fusion.6 = bf16[16,256,128]{2,1,0:T(8,128)(2,1)} fusion(bf16[16,256,128]{2,1,0:T(8,128)(2,1)} %bitcast.227, s32[16,256]{1,0:T(8,128)S(1)} %broadcast_subtract_fusion), kind=kOutput, calls=%fused_computation.8 | convolution fusion | flops 270008320 | bytes 2113536 | tf_op jit(solution)/shard_map/lpq,lqc->lpc/dot_general | solution.py:80
  4.5 5.7 %all-to-all-start = ((bf16[16,256,128]{2,1,0:T(8,128)(2,1)}), bf16[16,256,128]{2,1,0:T(8,128)(2,1)S(1)}, u32[]{:S(2)}, u32[]{:S(2)}) async-start(bf16[16,256,128]{2,1,0:T(8,128)(2,1)} %fusion.6), calls=%async_computation | async-start | bytes 2097152 | tf_op jit(solution)/shard_map/all_to_all | solution.py:89
  10.3 2.1 %fusion.2 = f32[16,256,8]{1,2,0:T(8,128)} fusion(f32[8,16,256]{2,0,1:T(8,128)S(1)} %bitcast.228, s32[16,256]{1,0:T(8,128)S(1)} %broadcast_subtract_fusion), kind=kOutput, calls=%fused_computation.3 | convolution fusion | flops 101711872 | bytes 278528 | tf_op jit(solution)/shard_map/dlq,lpq->ldp/dot_general | solution.py:87
  20.8 2.2 %all-to-all-done = bf16[16,256,128]{2,1,0:T(8,128)(2,1)S(1)} async-done(((bf16[16,256,128]{2,1,0:T(8,128)(2,1)}), bf16[16,256,128]{2,1,0:T(8,128)(2,1)S(1)}, u32[]{:S(2)}, u32[]{:S(2)}) %all-to-all-start) | async-done | bytes 1048608 | tf_op jit(solution)/shard_map/all_to_all | solution.py:89
  23.1 2.3 %fusion.11 = f32[4,128,512]{2,1,0:T(8,128)} fusion(bf16[4,4,32,8,128]{4,3,2,1,0:T(8,128)(2,1)S(1)} %bitcast.220, bf16[16,256,128]{2,1,0:T(8,128)(2,1)} %param.11, s32[]{:T(128)S(6)} %select_n.108), kind=kOutput, calls=%fused_computation.33 | convolution fusion | flops 134217728 | bytes 2359300 | tf_op jit(solution)/shard_map/lpr,lpc->lrc/dot_general | solution.py:33
  25.3 2.5 %copy.46 = f32[4,128,512]{1,0,2:T(4,128)} copy(f32[4,128,512]{2,1,0:T(8,128)} %fusion.11) | data formatting | bytes 2097152 | tf_op jit(solution)/shard_map/lpr,lpc->lrc/dot_general | solution.py:33
  27.9 5.7 %all-to-all-start.2 = ((f32[4,128,512]{1,0,2:T(4,128)}), f32[4,128,512]{1,0,2:T(4,128)}, u32[]{:S(2)}, u32[]{:S(2)}) async-start(f32[4,128,512]{1,0,2:T(4,128)} %copy.46), calls=%async_computation.2 | async-start | bytes 2097152 | tf_op jit(solution)/shard_map/all_to_all | solution.py:96
  35.0 3.9 %fusion.13 = f32[4,256,512]{2,1,0:T(8,128)} fusion(bf16[4,4,32,8,128]{4,3,2,1,0:T(8,128)(2,1)S(1)} %bitcast.221, f32[256,256]{1,0:T(8,128)S(1)} %fusion.45, f32[4,256]{1,0:T(4,128)} %get-tuple-element.19, f32[4,256]{1,0:T(4,128)} %get-tuple-element.20, f32[4,256]{1,0:T(4,128)S(1)} %get-tuple-element.21, f32[4,256]{1,0:T(4,128)S(1)} %get-tuple-element.22, ...), kind=kOutput, calls=%fused_computation.35 | convolution fusion | flops 275251200 | bytes 3440640 | tf_op jit(solution)/shard_map/lpq,lqc->lpc/dot_general | solution.py:32
  38.8 2.9 %copy.43 = f32[4,256,512]{1,0,2:T(4,128)} copy(f32[4,256,512]{2,1,0:T(8,128)} %fusion.13) | data formatting | bytes 4194304 | tf_op jit(solution)/shard_map/lpq,lqc->lpc/dot_general | solution.py:32
  41.7 3.9 %all-to-all-done.2 = f32[4,128,512]{1,0,2:T(4,128)} async-done(((f32[4,128,512]{1,0,2:T(4,128)}), f32[4,128,512]{1,0,2:T(4,128)}, u32[]{:S(2)}, u32[]{:S(2)}) %all-to-all-start.2) | async-done | bytes 1048608 | tf_op jit(solution)/shard_map/all_to_all | solution.py:96
  45.6 5.9 %all-to-all-start.1 = ((f32[4,256,512]{1,0,2:T(4,128)}), f32[4,256,512]{1,0,2:T(4,128)}, u32[]{:S(2)}, u32[]{:S(2)}) async-start(f32[4,256,512]{1,0,2:T(4,128)} %copy.43), calls=%async_computation.1 | async-start | bytes 4194304 | tf_op jit(solution)/shard_map/all_to_all | solution.py:95
  56.7 1.6 %convolution_bitcast_fusion.11 = f32[128,128]{0,1:T(8,128)} fusion(f32[128,128,1]{1,0,2:T(8,128)} %fusion.65, bf16[31,128,128]{2,1,0:T(8,128)(2,1)S(1)} %copy-done.2), kind=kOutput, calls=%fused_computation.29 | convolution fusion | flops 25165824 | bytes 163840 | tf_op jit(solution)/shard_map/dot_general | solution.py:45
  61.7 2.7 %collective-permute-start.3 = (f32[128,128]{1,0:T(8,128)S(1)}, f32[128,128]{1,0:T(8,128)S(1)}, u32[]{:S(2)}, u32[]{:S(2)}) collective-permute-start(f32[128,128]{1,0:T(8,128)S(1)} %fusion.85), channel_id=1, source_target_pairs={{0,8},{8,0},{4,12},{12,4},{16,24},{24,16},{20,28},{28,20},{32,40},... | collective-permute-start | bytes 196616 | tf_op jit(solution)/shard_map/ppermute | solution.py:17
  67.2 3.4 %collective-permute-start.5 = (f32[128,128]{1,0:T(8,128)S(1)}, f32[128,128]{1,0:T(8,128)S(1)}, u32[]{:S(2)}, u32[]{:S(2)}) collective-permute-start(f32[128,128]{1,0:T(8,128)S(1)} %fusion.81), channel_id=1, source_target_pairs={{0,16},{16,0},{4,20},{20,4},{8,24},{24,8},{12,28},{28,12},{32,48},... | collective-permute-start | bytes 196616 | tf_op jit(solution)/shard_map/ppermute | solution.py:17
  74.4 6.9 %collective-permute-start.7 = (f32[128,128]{1,0:T(8,128)}, f32[128,128]{1,0:T(8,128)}, u32[]{:S(2)}, u32[]{:S(2)}) collective-permute-start(f32[128,128]{1,0:T(8,128)} %fusion.77), channel_id=1, source_target_pairs={{0,32},{32,0},{4,36},{36,4},{8,40},{40,8},{12,44},{44,12},{16,48},... | collective-permute-start | bytes 196616 | tf_op jit(solution)/shard_map/ppermute | solution.py:17
  82.5 2.6 %copy.48 = f32[8,2,128,128]{3,2,1,0:T(8,128)} copy(f32[8,2,128,128]{2,3,0,1:T(8,128)} %pad_maximum_fusion) | data formatting | bytes 2097152 | tf_op jit(solution)/shard_map/stack | solution.py:53
  92.2 3.1 %collective-permute-start.10 = (f32[128,128]{1,0:T(8,128)S(1)}, f32[128,128]{1,0:T(8,128)S(1)}, u32[]{:S(2)}, u32[]{:S(2)}) collective-permute-start(f32[128,128]{1,0:T(8,128)S(1)} %add.223), channel_id=1, source_target_pairs={{0,128},{128,0},{4,132},{132,4},{8,136},{136,8},{12,140},{140,12},... | collective-permute-start | bytes 196616 | tf_op jit(solution)/shard_map/ppermute | solution.py:17
  97.4 2.1 %collective-permute-start.4 = (f32[128,128]{1,0:T(8,128)}, f32[128,128]{1,0:T(8,128)S(1)}, u32[]{:S(2)}, u32[]{:S(2)}) collective-permute-start(f32[128,128]{1,0:T(8,128)} %copy-done.13), channel_id=1, source_target_pairs={{0,16},{16,0},{4,20},{20,4},{8,24},{24,8},{12,28},{28,12},{32,48},... | collective-permute-start | bytes 196616 | tf_op jit(solution)/shard_map/ppermute | solution.py:17
  99.4 3.3 %collective-permute-start.6 = (f32[128,128]{1,0:T(8,128)}, f32[128,128]{1,0:T(8,128)S(1)}, u32[]{:S(2)}, u32[]{:S(2)}) collective-permute-start(f32[128,128]{1,0:T(8,128)} %copy-done.14), channel_id=1, source_target_pairs={{0,32},{32,0},{4,36},{36,4},{8,40},{40,8},{12,44},{44,12},{16,48},... | collective-permute-start | bytes 196616 | tf_op jit(solution)/shard_map/ppermute | solution.py:17
  104.3 2.7 %collective-permute-done.8 = f32[128,128]{1,0:T(8,128)S(1)} collective-permute-done((f32[128,128]{1,0:T(8,128)S(1)}, f32[128,128]{1,0:T(8,128)S(1)}, u32[]{:S(2)}, u32[]{:S(2)}) %collective-permute-start.8) | collective-permute-done | bytes 65568 | tf_op jit(solution)/shard_map/ppermute | solution.py:17
  111.0 1.7 %convolution_add_fusion.5 = f32[128,128]{1,0:T(8,128)} fusion(f32[128,128]{1,0:T(8,128)S(1)} %convolution_bitcast_fusion.10, f32[128,128]{0,1:T(8,128)} %collective-permute-done, bf16[128,128]{1,0:T(8,128)(2,1)S(1)} %get-tuple-element.5, bf16[128,128]{0,1:T(8,128)(2,1)S(1)} %copy-done.17, pred[]{:T(512)S(6)} %eq.49), kind=kOutput, calls=%fused_computation.30 | convolution fusion | flops 25198592 | bytes 262145 | tf_op jit(solution)/shard_map/dot_general | solution.py:45
  117.0 2.2 %fusion.7 = f32[16,128,128]{1,2,0:T(8,128)} fusion(f32[16,128,128]{1,2,0:T(8,128)S(1)} %copy.61, f32[16,128,128]{1,2,0:T(8,128)S(1)} %bitcast.219, bf16[31,128,128]{2,1,0:T(8,128)(2,1)S(1)} %copy-done.3), kind=kOutput, calls=%fused_computation.10 | convolution fusion | flops 402915328 | bytes 3670016 | tf_op jit(solution)/shard_map/nrs,nsc->nrc/dot_general | solution.py:41
  119.2 2.1 %copy.44 = f32[4,256,4,128]{1,3,0,2:T(8,128)S(1)} copy(f32[4,256,4,128]{1,0,3,2:T(4,128)} %bitcast.5) | data formatting | bytes 4194304 | tf_op jit(solution)/shard_map/all_to_all | solution.py:95
  122.4 3.6 %fusion = f32[16,256,128]{2,1,0:T(8,128)} fusion(f32[16,256,128]{1,2,0:T(8,128)S(1)} %bitcast_add_fusion, s32[16,256]{1,0:T(8,128)S(1)} %broadcast_subtract_fusion), kind=kOutput, calls=%fused_computation.1 | convolution fusion | flops 1611661312 | bytes 4210688 | tf_op jit(solution)/shard_map/lpq,lpc->lqc/dot_general | solution.py:147
  (124 shorter events, 46.9 us)
Async XLA Ops:
  0.0 17.5 %copy-start = (bf16[62,128,128]{2,1,0:T(8,128)(2,1)S(1)}, bf16[62,128,128]{2,1,0:T(8,128)(2,1)}, u32[]{:S(2)}) copy-start(bf16[62,128,128]{2,1,0:T(8,128)(2,1)} %param.14) | copy-start | bytes 6094852
  4.5 18.5 %all-to-all-start = ((bf16[16,256,128]{2,1,0:T(8,128)(2,1)}), bf16[16,256,128]{2,1,0:T(8,128)(2,1)S(1)}, u32[]{:S(2)}, u32[]{:S(2)}) async-start(bf16[16,256,128]{2,1,0:T(8,128)(2,1)} %fusion.6), calls=%async_computation | async-start | bytes 2097152 | tf_op jit(solution)/shard_map/all_to_all | solution.py:89
  13.2 14.7 %copy-start.7 = (bf16[128,128]{1,0:T(8,128)(2,1)}, bf16[128,128]{1,0:T(8,128)(2,1)S(1)}, u32[]{:S(2)}) copy-start(bf16[128,128]{1,0:T(8,128)(2,1)S(1)} %get-tuple-element.7) | copy-start | bytes 98308
  13.2 14.7 %copy-start.9 = (bf16[128,128]{1,0:T(8,128)(2,1)}, bf16[128,128]{1,0:T(8,128)(2,1)S(1)}, u32[]{:S(2)}) copy-start(bf16[128,128]{1,0:T(8,128)(2,1)S(1)} %get-tuple-element.6) | copy-start | bytes 98308
  13.2 14.7 %copy-start.10 = (bf16[128,128]{1,0:T(8,128)(2,1)}, bf16[128,128]{1,0:T(8,128)(2,1)S(1)}, u32[]{:S(2)}) copy-start(bf16[128,128]{1,0:T(8,128)(2,1)S(1)} %get-tuple-element.10) | copy-start | bytes 98308
  27.9 17.7 %all-to-all-start.2 = ((f32[4,128,512]{1,0,2:T(4,128)}), f32[4,128,512]{1,0,2:T(4,128)}, u32[]{:S(2)}, u32[]{:S(2)}) async-start(f32[4,128,512]{1,0,2:T(4,128)} %copy.46), calls=%async_computation.2 | async-start | bytes 2097152 | tf_op jit(solution)/shard_map/all_to_all | solution.py:96
  45.6 73.6 %all-to-all-start.1 = ((f32[4,256,512]{1,0,2:T(4,128)}), f32[4,256,512]{1,0,2:T(4,128)}, u32[]{:S(2)}, u32[]{:S(2)}) async-start(f32[4,256,512]{1,0,2:T(4,128)} %copy.43), calls=%async_computation.1 | async-start | bytes 4194304 | tf_op jit(solution)/shard_map/all_to_all | solution.py:95
  58.3 1.9 %collective-permute-start.1 = (f32[128,128]{0,1:T(8,128)}, f32[128,128]{0,1:T(8,128)}, u32[]{:S(2)}, u32[]{:S(2)}) collective-permute-start(f32[128,128]{0,1:T(8,128)} %convolution_bitcast_fusion.11), channel_id=1, source_target_pairs={{0,4},{4,0},{8,12},{12,8},{16,20},{20,16},{24,28},{28,24},{32,36},... | collective-permute-start | bytes 196616 | tf_op jit(solution)/shard_map/ppermute | solution.py:17
  58.3 52.7 %collective-permute-start = (f32[128,128]{0,1:T(8,128)}, f32[128,128]{0,1:T(8,128)}, u32[]{:S(2)}, u32[]{:S(2)}) collective-permute-start(f32[128,128]{0,1:T(8,128)} %bitcast.44), channel_id=1, source_target_pairs={{0,4},{4,0},{8,12},{12,8},{16,20},{20,16},{24,28},{28,24},{32,36},... | collective-permute-start | bytes 196616 | tf_op jit(solution)/shard_map/ppermute | solution.py:17
  61.7 4.9 %collective-permute-start.3 = (f32[128,128]{1,0:T(8,128)S(1)}, f32[128,128]{1,0:T(8,128)S(1)}, u32[]{:S(2)}, u32[]{:S(2)}) collective-permute-start(f32[128,128]{1,0:T(8,128)S(1)} %fusion.85), channel_id=1, source_target_pairs={{0,8},{8,0},{4,12},{12,4},{16,24},{24,16},{20,28},{28,20},{32,40},... | collective-permute-start | bytes 196616 | tf_op jit(solution)/shard_map/ppermute | solution.py:17
  67.2 6.2 %collective-permute-start.5 = (f32[128,128]{1,0:T(8,128)S(1)}, f32[128,128]{1,0:T(8,128)S(1)}, u32[]{:S(2)}, u32[]{:S(2)}) collective-permute-start(f32[128,128]{1,0:T(8,128)S(1)} %fusion.81), channel_id=1, source_target_pairs={{0,16},{16,0},{4,20},{20,4},{8,24},{24,8},{12,28},{28,12},{32,48},... | collective-permute-start | bytes 196616 | tf_op jit(solution)/shard_map/ppermute | solution.py:17
  74.4 12.4 %collective-permute-start.7 = (f32[128,128]{1,0:T(8,128)}, f32[128,128]{1,0:T(8,128)}, u32[]{:S(2)}, u32[]{:S(2)}) collective-permute-start(f32[128,128]{1,0:T(8,128)} %fusion.77), channel_id=1, source_target_pairs={{0,32},{32,0},{4,36},{36,4},{8,40},{40,8},{12,44},{44,12},{16,48},... | collective-permute-start | bytes 196616 | tf_op jit(solution)/shard_map/ppermute | solution.py:17
  86.7 22.7 %copy-start.8 = (bf16[128,128]{1,0:T(8,128)(2,1)S(1)}, bf16[128,128]{1,0:T(8,128)(2,1)}, u32[]{:S(2)}) copy-start(bf16[128,128]{1,0:T(8,128)(2,1)} %copy-done.7) | copy-start | bytes 98308
  86.7 22.7 %copy-start.19 = (bf16[128,128]{0,1:T(8,128)(2,1)S(1)}, bf16[128,128]{0,1:T(8,128)(2,1)}, u32[]{:S(2)}) copy-start(bf16[128,128]{0,1:T(8,128)(2,1)} %copy.53) | copy-start | bytes 98308
  86.7 23.1 %copy-start.18 = (bf16[128,128]{0,1:T(8,128)(2,1)S(1)}, bf16[128,128]{0,1:T(8,128)(2,1)}, u32[]{:S(2)}) copy-start(bf16[128,128]{0,1:T(8,128)(2,1)} %copy.52) | copy-start | bytes 98308
  86.7 24.3 %copy-start.17 = (bf16[128,128]{0,1:T(8,128)(2,1)S(1)}, bf16[128,128]{0,1:T(8,128)(2,1)}, u32[]{:S(2)}) copy-start(bf16[128,128]{0,1:T(8,128)(2,1)} %copy.51) | copy-start | bytes 98308
  87.9 4.4 %collective-permute-start.9 = (f32[128,128]{1,0:T(8,128)S(1)}, f32[128,128]{1,0:T(8,128)S(1)}, u32[]{:S(2)}, u32[]{:S(2)}) collective-permute-start(f32[128,128]{1,0:T(8,128)S(1)} %fusion.73), channel_id=1, source_target_pairs={{0,64},{64,0},{4,68},{68,4},{8,72},{72,8},{12,76},{76,12},{16,80},... | collective-permute-start | bytes 196616 | tf_op jit(solution)/shard_map/ppermute | solution.py:17
  92.2 10.5 %collective-permute-start.10 = (f32[128,128]{1,0:T(8,128)S(1)}, f32[128,128]{1,0:T(8,128)S(1)}, u32[]{:S(2)}, u32[]{:S(2)}) collective-permute-start(f32[128,128]{1,0:T(8,128)S(1)} %add.223), channel_id=1, source_target_pairs={{0,128},{128,0},{4,132},{132,4},{8,136},{136,8},{12,140},{140,12},... | collective-permute-start | bytes 196616 | tf_op jit(solution)/shard_map/ppermute | solution.py:17
  96.9 16.7 %copy-start.15 = (f32[1,1,128,128]{2,3,1,0:T(8,128)S(1)}, f32[1,1,128,128]{2,3,1,0:T(8,128)}, u32[]{:S(2)}) copy-start(f32[1,1,128,128]{2,3,1,0:T(8,128)} %convolution_bitcast_fusion.12) | copy-start | bytes 196612
  96.9 16.7 %copy-start.16 = (f32[1,1,128,128]{2,3,1,0:T(8,128)S(1)}, f32[1,1,128,128]{2,3,1,0:T(8,128)}, u32[]{:S(2)}) copy-start(f32[1,1,128,128]{2,3,1,0:T(8,128)} %convolution_bitcast_fusion.13) | copy-start | bytes 196612
  96.9 12.8 %collective-permute-start.2 = (f32[128,128]{0,1:T(8,128)}, f32[128,128]{0,1:T(8,128)S(1)}, u32[]{:S(2)}, u32[]{:S(2)}) collective-permute-start(f32[128,128]{0,1:T(8,128)} %copy-done.12), channel_id=1, source_target_pairs={{0,8},{8,0},{4,12},{12,4},{16,24},{24,16},{20,28},{28,20},{32,40},... | collective-permute-start | bytes 196616 | tf_op jit(solution)/shard_map/ppermute | solution.py:17
  97.4 12.0 %collective-permute-start.4 = (f32[128,128]{1,0:T(8,128)}, f32[128,128]{1,0:T(8,128)S(1)}, u32[]{:S(2)}, u32[]{:S(2)}) collective-permute-start(f32[128,128]{1,0:T(8,128)} %copy-done.13), channel_id=1, source_target_pairs={{0,16},{16,0},{4,20},{20,4},{8,24},{24,8},{12,28},{28,12},{32,48},... | collective-permute-start | bytes 196616 | tf_op jit(solution)/shard_map/ppermute | solution.py:17
  99.4 8.8 %collective-permute-start.6 = (f32[128,128]{1,0:T(8,128)}, f32[128,128]{1,0:T(8,128)S(1)}, u32[]{:S(2)}, u32[]{:S(2)}) collective-permute-start(f32[128,128]{1,0:T(8,128)} %copy-done.14), channel_id=1, source_target_pairs={{0,32},{32,0},{4,36},{36,4},{8,40},{40,8},{12,44},{44,12},{16,48},... | collective-permute-start | bytes 196616 | tf_op jit(solution)/shard_map/ppermute | solution.py:17
  102.8 4.3 %collective-permute-start.8 = (f32[128,128]{1,0:T(8,128)S(1)}, f32[128,128]{1,0:T(8,128)S(1)}, u32[]{:S(2)}, u32[]{:S(2)}) collective-permute-start(f32[128,128]{1,0:T(8,128)S(1)} %add.219), channel_id=1, source_target_pairs={{0,64},{64,0},{4,68},{68,4},{8,72},{72,8},{12,76},{76,12},{16,80},... | collective-permute-start | bytes 196616 | tf_op jit(solution)/shard_map/ppermute | solution.py:17
  (11 other events, 38.5 us)
where the time goes:
time: 128 us; the launch traced here: 126 us
  matrix products  41.6 us (32%)
  starting transfers between devices  41.5 us (32%)
  local copies, waits for them, and re-layouts  26.5 us (21%)
  waiting for transfers between devices  12.7 us (10%)
  other arithmetic  3.02 us (2%)
    ppermute x11, starting transfers between devices, swapped(): return lax.ppermute(block, axis, route)  24.3 us
    dot_general x17, matrix products, apply_single(): jnp.dot(matrix.astype(jnp.float32), vector, precision=lax.Precision.HIGHEST)  10.7 us
    ppermute x11, waiting for transfers between devices, swapped(): return lax.ppermute(block, axis, route)  6.6 us
    all_to_all x1, starting transfers between devices, local(): lax.all_to_all(direct_part, 'rhs', split_axis=2, concat_axis=0, tiled=True)  5.88 us
    all_to_all x1, starting transfers between devices, local(): lax.all_to_all(upward_part, 'rhs', split_axis=2, concat_axis=0, tiled=True)  5.69 us
    all_to_all x1, starting transfers between devices, local(): lax.all_to_all(ordered, 'rhs', split_axis=0, concat_axis=2, tiled=True)  5.67 us
    dot_general x4, matrix products, apply_batch(): jnp.einsum('nrs,nsc->nrc', mats.astype(jnp.float32), vectors, precision=h...  5.35 us
    squeeze x7, local copies, waits for them, and re-layouts, local(): lax.dynamic_index_in_dim(top_coupling, coupling_index, 0, keepdims=False)  5.11 us
  transfers between devices with their start and end apart: 14, of which 6 were waited for; matrix products, arithmetic and copies ran while one was open for 43% of the time, Pallas kernels for 0%

commit v1 on v0

v1 whole, which is shorter than its diff:
```python
import functools
import math

import jax
import jax.numpy as jnp
from jax import lax
from jax.experimental import pallas as pl
from jax.experimental.pallas import tpu as pltpu
from jax.sharding import PartitionSpec as P

MESH = pl.DeviceIdType.MESH
BF, F32 = jnp.bfloat16, jnp.float32
LEAF, RANK, COLS, LEAVES = 256, 128, 128, 16
HALF = COLS // 2
NZ, NX = 8, 4
SCALE = math.sqrt(0.1 * math.log2(math.e))
CHUNK = 4


def nn(a, b):
    return lax.dot_general(a, b, (((1,), (0,)), ((), ())), preferred_element_type=F32)


def nt(a, b):
    return lax.dot_general(a, b, (((1,), (1,)), ((), ())), preferred_element_type=F32)


def tn(a, b):
    return lax.dot_general(a, b, (((0,), (0,)), ((), ())), preferred_element_type=F32)


def split(u):
    hi = u.astype(BF)
    return hi, (u - hi.astype(F32)).astype(BF)


def times(u, mat):
    hi, lo = split(u)
    return nn(hi, mat) + nn(lo, mat)


def times_t(u, mat):
    hi, lo = split(u)
    return nt(hi, mat) + nt(lo, mat)


def kernel(
    points, charges, order, basis, trans, coup, top_t, top_c, out,
    pts_v, q_v, ord_v, bas_v, tr_v, cp_v, t5_v, t6_v, t7_v, t8_v, c_v,
    bs_v, uhi, ulo, side_v, lhs_v, rhs_v,
    u4_v, u4p_v, rp_v, zbuf, xbuf, u6_v, u7_v, d5_v, down_v,
    in_sem, ck_sem, cs_s, cs_r, zs, zr, xs, xr, ds_s, ds_r,
):
    me, col = lax.axis_index("leaf"), lax.axis_index("rhs")
    core = me % 2
    z = (me // 2) % NZ
    x = me // (2 * NZ)
    chip = me // 2

    def at(xx, zz, cc):
        return ((xx * NZ + zz) * 2 + cc, col)

    partner = at(x, z, 1 - core)
    zpeers = [at(x, (z + k) % NZ, core) for k in range(1, NZ)]
    xpeers = [at((x + k) % NX, z, core) for k in range(1, NX)]

    rows = CHUNK * LEAF
    order_cp = pltpu.make_async_copy(order, ord_v, in_sem.at[0])
    order_cp.start()

    def chunk_copies(c):
        return (
            pltpu.make_async_copy(basis.at[pl.ds(c * CHUNK, CHUNK)], bas_v.at[pl.ds(c * CHUNK, CHUNK)], ck_sem.at[0, c]),
            pltpu.make_async_copy(charges.at[pl.ds(c * rows, rows)], q_v.at[pl.ds(c * rows, rows)], ck_sem.at[1, c]),
        )

    for cp in chunk_copies(0):
        cp.start()
    trans_cp = pltpu.make_async_copy(trans, tr_v, in_sem.at[1])
    trans_cp.start()
    for c in range(1, LEAVES // CHUNK):
        for cp in chunk_copies(c):
            cp.start()
    late = [
        pltpu.make_async_copy(points, pts_v, in_sem.at[2]),
        pltpu.make_async_copy(coup, cp_v, in_sem.at[3]),
        pltpu.make_async_copy(top_t.at[pl.ds(x * 8, 8)], t5_v, in_sem.at[4]),
        pltpu.make_async_copy(top_t.at[pl.ds(32 + x * 4, 4)], t6_v, in_sem.at[5]),
        pltpu.make_async_copy(top_t.at[pl.ds(48 + x * 2, 2)], t7_v, in_sem.at[6]),
        pltpu.make_async_copy(top_t.at[pl.ds(56, 4)], t8_v, in_sem.at[7]),
        pltpu.make_async_copy(top_c.at[chip], c_v.at[0], in_sem.at[8]),
        pltpu.make_async_copy(top_c.at[32 + chip // 2], c_v.at[1], in_sem.at[9]),
        pltpu.make_async_copy(top_c.at[48 + chip // 4], c_v.at[2], in_sem.at[10]),
        pltpu.make_async_copy(top_c.at[56 + x], c_v.at[3], in_sem.at[11]),
        pltpu.make_async_copy(top_c.at[60 + x // 2], c_v.at[4], in_sem.at[12]),
        pltpu.make_async_copy(top_c.at[62], c_v.at[5], in_sem.at[13]),
    ]
    for cp in late:
        cp.start()

    barrier = pltpu.get_barrier_semaphore()
    peers = [partner] + zpeers + xpeers
    for peer in peers:
        pl.semaphore_signal(barrier, inc=1, device_id=peer, device_id_type=MESH)

    slot = lax.broadcasted_iota(jnp.int32, (LEAF, LEAF), 0)
    order_cp.wait()

    def put(node, u):
        hi, lo = split(u)
        uhi[node] = hi
        ulo[node] = lo
        return hi, lo

    def parent(left, right, mats):
        mats = mats.reshape(2 * RANK, RANK)
        hi = jnp.concatenate((left[0], right[0]), axis=1)
        lo = jnp.concatenate((left[1], right[1]), axis=1)
        return nn(hi, mats) + nn(lo, mats)

    def chunk(c, carry):
        for cp in chunk_copies(c):
            cp.wait()

        @pl.when(c == 0)
        def _():
            trans_cp.wait()

        ups = []
        for i in range(CHUNK):
            leaf = c * CHUNK + i
            where = ord_v[pl.ds(pl.multiple_of(leaf * LEAF, LEAF), LEAF)] & (LEAF - 1)
            pick = jnp.where(slot == where[None, :], 1.0, 0.0).astype(BF)
            own = nn(pick, bas_v[leaf]).astype(BF)
            bs_v[leaf] = own
            u = tn(q_v[pl.ds(pl.multiple_of(leaf * LEAF, LEAF), LEAF)], own)
            ups.append(put(leaf, u))
        next_ups = []
        for i in range(2):
            node = 2 * c + i
            u = parent(ups[2 * i], ups[2 * i + 1], tr_v[pl.ds(2 * node, 2)])
            next_ups.append(put(16 + node, u))
        u = parent(next_ups[0], next_ups[1], tr_v[pl.ds(16 + 2 * c, 2)])
        put(24 + c, u)
        return carry

    lax.fori_loop(0, LEAVES // CHUNK, chunk, 0)

    def read(node):
        return uhi[node], ulo[node]

    for i in range(2):
        put(28 + i, parent(read(24 + 2 * i), read(25 + 2 * i), tr_v[24 + 2 * i : 26 + 2 * i]))
    u4 = parent(read(28), read(29), tr_v[28:30])
    u4_v[...] = u4

    pl.semaphore_wait(barrier, len(peers))
    mine_rows = pl.ds(pl.multiple_of(core * HALF, HALF), HALF)
    other_rows = pl.ds(pl.multiple_of((1 - core) * HALF, HALF), HALF)

    def remote(src, dst, send, recv, peer):
        return pltpu.make_async_remote_copy(
            src_ref=src, dst_ref=dst, send_sem=send, recv_sem=recv, device_id=peer, device_id_type=MESH
        )

    swaps = [
        remote(u4_v.at[other_rows], u4p_v.at[other_rows], cs_s.at[0], cs_r.at[0], partner),
        remote(tr_v.at[30], rp_v, cs_s.at[1], cs_r.at[1], partner),
        remote(u4_v.at[mine_rows], u4p_v.at[mine_rows], cs_s.at[2], cs_r.at[2], partner),
    ]
    for cp in swaps:
        cp.start()
    for cp in late:
        cp.wait()
    swaps[0].wait_recv()
    swaps[1].wait_recv()
    u5 = times(u4_v[mine_rows], tr_v[30]) + times(u4p_v[mine_rows], rp_v[...])
    zbuf[z] = u5.astype(BF)
    zsends = [remote(zbuf.at[z], zbuf.at[z], zs.at[k], zr.at[k], zpeers[k]) for k in range(NZ - 1)]
    for k in (3, 2, 4, 1, 5, 0, 6):
        zsends[k].start()

    xs_all = pts_v[...] * SCALE
    h = xs_all.astype(BF).astype(F32)
    rest = xs_all - h
    m = rest.astype(BF).astype(F32)
    low = rest - m
    norm = jnp.sum(xs_all * xs_all, axis=0, keepdims=True)
    nh = norm.astype(BF).astype(F32)
    nrest = norm - nh
    nm = nrest.astype(BF).astype(F32)
    nl = nrest - nm
    wide = norm.shape[1]
    one = jnp.ones((1, wide), F32)
    zero = jnp.zeros((2, wide), F32)
    pad = jnp.zeros((8, wide), F32)
    lhs_v[...] = jnp.concatenate((h, h, m, m, h, low, nh, nm, nl, one, one, one, zero, pad), axis=0).astype(BF)
    rhs_v[...] = jnp.concatenate(
        (2 * h, 2 * m, 2 * h, 2 * m, 2 * low, 2 * h, -one, -one, -one, -nh, -nm, -nl, zero, pad), axis=0
    ).astype(BF)

    def direct(c, carry):
        for i in range(2):
            where = pl.ds(pl.multiple_of((2 * c + i) * LEAF, LEAF), LEAF)
            dist = tn(lhs_v[:, where], rhs_v[:, where])
            q = q_v[where]
            out[where, :] = nn(jnp.exp2(dist).astype(BF), q) + 0.5 * q.astype(F32)
        return carry

    lax.fori_loop(0, LEAVES // 2, direct, 0)

    def sides(pair, carry):
        mat = cp_v[pair]
        left, right = 2 * pair, 2 * pair + 1
        side_v[left] = nt(uhi[right], mat) + nt(ulo[right], mat)
        side_v[right] = nn(uhi[left], mat) + nn(ulo[left], mat)
        return carry

    lax.fori_loop(0, 15, sides, 0)

    swaps[2].wait_recv()

    def towards(index, bit):
        mat = c_v[index]
        return jnp.where(bit == 0, mat.astype(F32).T, mat.astype(F32)).astype(BF)

    side4 = times(u4p_v[...], towards(0, core))

    for cp in zsends:
        cp.wait_recv()
    for i in range(4):
        u6_v[i] = nn(jnp.concatenate((zbuf[2 * i], zbuf[2 * i + 1]), axis=1), t5_v[2 * i : 2 * i + 2].reshape(2 * RANK, RANK))
    for i in range(2):
        u7_v[i] = parent(split(u6_v[2 * i]), split(u6_v[2 * i + 1]), t6_v[2 * i : 2 * i + 2])
    u8 = parent(split(u7_v[0]), split(u7_v[1]), t7_v[...])
    xbuf[x] = u8.astype(BF)
    xsends = [remote(xbuf.at[x], xbuf.at[x], xs.at[k], xr.at[k], xpeers[k]) for k in range(NX - 1)]
    for k in (1, 0, 2):
        xsends[k].start()
    sib = z + 1 - 2 * (z % 2)
    side5 = nn(zbuf[sib], towards(1, z % 2))
    half_z = z // 2
    sib = half_z + 1 - 2 * (half_z % 2)
    side6 = times(u6_v[sib], towards(2, half_z % 2))
    quarter_z = z // 4
    side7 = times(u7_v[1 - quarter_z], towards(3, quarter_z))
    m8, m9 = towards(4, x % 2), towards(5, x // 2)

    for cp in xsends:
        cp.wait_recv()
    far = 2 - 2 * (x // 2)
    u9 = nn(xbuf[far], t8_v[far]) + nn(xbuf[far + 1], t8_v[far + 1])
    sib = x + 1 - 2 * (x % 2)
    d9 = times(u9, m9)
    d8 = nn(xbuf[sib], m8) + times_t(d9, t8_v[x])
    d7 = side7 + times_t(d8, t7_v[quarter_z])
    d6 = side6 + times_t(d7, t6_v[half_z])
    d5_v[mine_rows] = side5 + times_t(d6, t5_v[z])
    back = remote(d5_v.at[mine_rows], d5_v.at[mine_rows], ds_s.at[0], ds_r.at[0], partner)
    back.start()
    back.wait_recv()

    down_v[30] = side4 + times_t(d5_v[...], tr_v[30])
    for count, start in ((2, 28), (4, 24), (8, 16)):
        above = start + count
        for i in range(count):
            down_v[start + i] = side_v[start + i] + times_t(down_v[above + i // 2], tr_v[start + i])

    def final(pair, carry):
        for i in range(2):
            leaf = 2 * pair + i
            where = pl.ds(pl.multiple_of(leaf * LEAF, LEAF), LEAF)
            down = side_v[leaf] + times_t(down_v[16 + pair], tr_v[leaf])
            hi, lo = split(down)
            own = bs_v[leaf]
            out[where, :] += nt(jnp.concatenate((own, own), axis=1), jnp.concatenate((hi, lo), axis=1))
        return carry

    lax.fori_loop(0, LEAVES // 2, final, 0)

    for cp in swaps + zsends + xsends + [back]:
        cp.wait_send()


def local(*args):
    vm = pltpu.VMEM
    dma = pltpu.SemaphoreType.DMA
    rows = LEAVES * LEAF
    return pl.pallas_call(
        kernel,
        out_shape=jax.ShapeDtypeStruct((rows, COLS), F32),
        in_specs=[pl.BlockSpec(memory_space=pl.ANY)] * 8,
        out_specs=pl.BlockSpec(memory_space=pltpu.VMEM),
        scratch_shapes=[
            vm((8, rows), F32),
            vm((rows, COLS), BF),
            vm((rows,), jnp.int32),
            vm((LEAVES, LEAF, RANK), BF),
            vm((31, RANK, RANK), BF),
            vm((15, RANK, RANK), BF),
            vm((8, RANK, RANK), BF),
            vm((4, RANK, RANK), BF),
            vm((2, RANK, RANK), BF),
            vm((4, RANK, RANK), BF),
            vm((6, RANK, RANK), BF),
            vm((LEAVES, LEAF, RANK), BF),
            vm((30, COLS, RANK), BF),
            vm((30, COLS, RANK), BF),
            vm((30, COLS, RANK), F32),
            vm((64, rows), BF),
            vm((64, rows), BF),
            vm((COLS, RANK), F32),
            vm((COLS, RANK), F32),
            vm((RANK, RANK), BF),
            vm((NZ, HALF, RANK), BF),
            vm((NX, HALF, RANK), BF),
            vm((4, HALF, RANK), F32),
            vm((2, HALF, RANK), F32),
            vm((COLS, RANK), F32),
            vm((31, COLS, RANK), F32),
            dma((14,)),
            dma((2, LEAVES // CHUNK)),
            dma((3,)),
            dma((3,)),
            dma((NZ - 1,)),
            dma((NZ - 1,)),
            dma((NX - 1,)),
            dma((NX - 1,)),
            dma((1,)),
            dma((1,)),
        ],
        compiler_params=pltpu.CompilerParams(
            collective_id=0, has_side_effects=True, vmem_limit_bytes=40 * 1024 * 1024
        ),
    )(*args)


def solution(mesh):
    placed = (
        P(None, "leaf"),
        P("leaf", "rhs"),
        P("leaf"),
        P("leaf", None, None),
        P("leaf", None, None),
        P("leaf", None, None),
        P(),
        P(),
    )
    return jax.shard_map(
        local, mesh=mesh, in_specs=placed, out_specs=P("leaf", "rhs"), check_vma=False
    )
```

time: 128 us -> 43 us (0.34)
  the two profiles are of different devices: /device:TPU:8 before, /device:TPU:1 now
where the time goes in v1:
time: 43 us; the launch traced here: 42.6 us
  Pallas kernels  31.8 us (74%)
  local copies, waits for them, and re-layouts  10.8 us (25%)
    pallas_call x1, Pallas kernels, local(): pl.pallas_call(kernel, out_shape=jax.ShapeDtypeStruct((rows, COLS), F32),...  31.8 us
    unnamed x17, local copies, waits for them, and re-layouts  10.8 us

profile of v1, /device:TPU:1, one launch (start us, length us, event | category | flops | bytes accessed | tf_op | source)
XLA Modules:
  0.0 42.6 jit_solution(12572741823903278356)
XLA Ops:
  0.0 0.0 copy-start
  0.0 1.6 %copy-done = bf16[63,128,128]{2,1,0:T(8,128)(2,1)S(1)} copy-done((bf16[63,128,128]{2,1,0:T(8,128)(2,1)S(1)}, bf16[63,128,128]{2,1,0:T(8,128)(2,1)}, u32[]{:S(2)}) %copy-start) | copy-done | bytes 2064408
  1.6 0.0 copy-start.1
  1.6 1.6 %copy-done.1 = bf16[62,128,128]{2,1,0:T(8,128)(2,1)S(1)} copy-done((bf16[62,128,128]{2,1,0:T(8,128)(2,1)S(1)}, bf16[62,128,128]{2,1,0:T(8,128)(2,1)}, u32[]{:S(2)}) %copy-start.1) | copy-done | bytes 2031640
  3.1 0.0 copy-start.2
  3.2 1.2 %copy-done.2 = bf16[4096,128]{1,0:T(8,128)(2,1)S(1)} copy-done((bf16[4096,128]{1,0:T(8,128)(2,1)S(1)}, bf16[4096,128]{1,0:T(8,128)(2,1)}, u32[]{:S(2)}) %copy-start.2) | copy-done | bytes 1048600
  4.4 0.0 copy-start.3
  4.4 1.2 %copy-done.3 = bf16[16,256,128]{2,1,0:T(8,128)(2,1)S(1)} copy-done((bf16[16,256,128]{2,1,0:T(8,128)(2,1)S(1)}, bf16[16,256,128]{2,1,0:T(8,128)(2,1)}, u32[]{:S(2)}) %copy-start.3) | copy-done | bytes 1048600
  5.6 0.0 copy-start.4
  5.6 1.2 %copy-done.4 = bf16[31,128,128]{2,1,0:T(8,128)(2,1)S(1)} copy-done((bf16[31,128,128]{2,1,0:T(8,128)(2,1)S(1)}, bf16[31,128,128]{2,1,0:T(8,128)(2,1)}, u32[]{:S(2)}) %copy-start.4) | copy-done | bytes 1015832
  6.8 0.0 copy-start.5
  6.8 1.0 %copy-done.5 = bf16[15,128,128]{2,1,0:T(8,128)(2,1)S(1)} copy-done((bf16[15,128,128]{2,1,0:T(8,128)(2,1)S(1)}, bf16[15,128,128]{2,1,0:T(8,128)(2,1)}, u32[]{:S(2)}) %copy-start.5) | copy-done | bytes 491544
  7.8 0.0 copy-start.6
  7.8 0.9 %copy-done.6 = f32[8,4096]{1,0:T(8,128)S(1)} copy-done((f32[8,4096]{1,0:T(8,128)S(1)}, f32[8,4096]{1,0:T(8,128)}, u32[]{:S(2)}) %copy-start.6) | copy-done | bytes 131096
  8.7 0.0 copy-start.7
  8.8 0.7 %copy-done.7 = s32[4096]{0:T(1024)S(1)} copy-done((s32[4096]{0:T(1024)S(1)}, s32[4096]{0:T(1024)}, u32[]{:S(2)}) %copy-start.7) | copy-done | bytes 16408
  9.5 31.8 %shard_map.82 = f32[4096,128]{1,0:T(8,128)S(1)} custom-call(f32[8,4096]{1,0:T(8,128)S(1)} %copy-done.6, bf16[4096,128]{1,0:T(8,128)(2,1)S(1)} %copy-done.2, s32[4096]{0:T(1024)S(1)} %copy-done.7, bf16[16,256,128]{2,1,0:T(8,128)(2,1)S(1)} %copy-done.3, bf16[31,128,128]{2,1,0:T(8,128)(2,1)S(1)} %copy-done.4, bf16[15,128,128]{2,1,0:T(8,128)(2,1)S(1)} %copy-done.5, ...), custom_call_target="tpu_custom_call" | custom-call | tf_op jit(solution)/shard_map/pallas_call | solution.py:289
  41.3 1.3 %copy.10 = f32[4096,128]{1,0:T(8,128)} copy(f32[4096,128]{1,0:T(8,128)S(1)} %shard_map.82) | data formatting | bytes 4194304
Async XLA Ops:
  0.0 1.6 %copy-start = (bf16[63,128,128]{2,1,0:T(8,128)(2,1)S(1)}, bf16[63,128,128]{2,1,0:T(8,128)(2,1)}, u32[]{:S(2)}) copy-start(bf16[63,128,128]{2,1,0:T(8,128)(2,1)} %top_c.1) | copy-start | bytes 6193156
  1.6 1.6 %copy-start.1 = (bf16[62,128,128]{2,1,0:T(8,128)(2,1)S(1)}, bf16[62,128,128]{2,1,0:T(8,128)(2,1)}, u32[]{:S(2)}) copy-start(bf16[62,128,128]{2,1,0:T(8,128)(2,1)} %top_t.1) | copy-start | bytes 6094852
  3.1 1.2 %copy-start.2 = (bf16[4096,128]{1,0:T(8,128)(2,1)S(1)}, bf16[4096,128]{1,0:T(8,128)(2,1)}, u32[]{:S(2)}) copy-start(bf16[4096,128]{1,0:T(8,128)(2,1)} %charges.1) | copy-start | bytes 3145732
  4.4 1.2 %copy-start.3 = (bf16[16,256,128]{2,1,0:T(8,128)(2,1)S(1)}, bf16[16,256,128]{2,1,0:T(8,128)(2,1)}, u32[]{:S(2)}) copy-start(bf16[16,256,128]{2,1,0:T(8,128)(2,1)} %basis.1) | copy-start | bytes 3145732
  5.6 1.2 %copy-start.4 = (bf16[31,128,128]{2,1,0:T(8,128)(2,1)S(1)}, bf16[31,128,128]{2,1,0:T(8,128)(2,1)}, u32[]{:S(2)}) copy-start(bf16[31,128,128]{2,1,0:T(8,128)(2,1)} %trans.1) | copy-start | bytes 3047428
  6.8 1.0 %copy-start.5 = (bf16[15,128,128]{2,1,0:T(8,128)(2,1)S(1)}, bf16[15,128,128]{2,1,0:T(8,128)(2,1)}, u32[]{:S(2)}) copy-start(bf16[15,128,128]{2,1,0:T(8,128)(2,1)} %coup.1) | copy-start | bytes 1474564
  7.8 0.9 %copy-start.6 = (f32[8,4096]{1,0:T(8,128)S(1)}, f32[8,4096]{1,0:T(8,128)}, u32[]{:S(2)}) copy-start(f32[8,4096]{1,0:T(8,128)} %points.1) | copy-start | bytes 393220
  8.7 0.7 %copy-start.7 = (s32[4096]{0:T(1024)S(1)}, s32[4096]{0:T(1024)}, u32[]{:S(2)}) copy-start(s32[4096]{0:T(1024)} %order.1) | copy-start | bytes 49156

commit v2 on v1

v2 whole, which is shorter than its diff:
```python
import functools
import math

import jax
import jax.numpy as jnp
from jax import lax
from jax.experimental import pallas as pl
from jax.experimental.pallas import tpu as pltpu
from jax.sharding import PartitionSpec as P

MESH = pl.DeviceIdType.MESH
BF, F32 = jnp.bfloat16, jnp.float32
LEAF, RANK, COLS, LEAVES = 256, 128, 128, 16
HALF = COLS // 2
NZ, NX = 8, 4
SCALE = math.sqrt(0.1 * math.log2(math.e))
GROUP = 8


def nn(a, b):
    return lax.dot_general(a, b, (((1,), (0,)), ((), ())), preferred_element_type=F32)


def nt(a, b):
    return lax.dot_general(a, b, (((1,), (1,)), ((), ())), preferred_element_type=F32)


def tn(a, b):
    return lax.dot_general(a, b, (((0,), (0,)), ((), ())), preferred_element_type=F32)


def split(u):
    hi = u.astype(BF)
    return hi, (u - hi.astype(F32)).astype(BF)


def beside(*parts):
    return jnp.concatenate(parts, axis=1)


def stacked(*parts):
    return jnp.concatenate(parts, axis=0)


def times(u, mat):
    return nn(beside(*u), stacked(mat, mat))


def times_t(u, mat):
    return nt(beside(*u), beside(mat, mat))


def mat_times(mat, u):
    both = nn(mat, beside(*u))
    return both[:, :RANK] + both[:, RANK:]


def kernel(
    points, charges, order, basis, trans, coup, top_t, top_c, out,
    pts_v, q_v, ord_v, bas_v, tr_v, cp_v, t5_v, t6_v, t7_v, t8_v, c_v,
    bs_v, uhi, ulo, side_v, lhs_v, rhs_v, e_v, pick_v,
    u4_v, u4p_v, rp_v, zbuf, xbuf, d5_v, q2_v, e2_v, h_v, m_v, d2_v,
    in_sem, cs_s, cs_r, zs, zr, xs, xr, ds_s, ds_r,
):
    me, col = lax.axis_index("leaf"), lax.axis_index("rhs")
    core = me % 2
    z = (me // 2) % NZ
    x = me // (2 * NZ)
    chip = me // 2

    def at(xx, zz, cc):
        return ((xx * NZ + zz) * 2 + cc, col)

    partner = at(x, z, 1 - core)
    zpeers = [at(x, (z + k) % NZ, core) for k in range(1, NZ)]
    xpeers = [at((x + k) % NX, z, cc) for k in range(1, NX) for cc in (core, 1 - core)]

    def load(src, dst, sem):
        cp = pltpu.make_async_copy(src, dst, in_sem.at[sem])
        cp.start()
        return cp

    order_cp = load(order, ord_v, 0)
    basis_cp = load(basis, bas_v, 1)
    charges_cp = load(charges, q_v, 2)
    trans_cp = load(trans, tr_v, 3)
    late = [
        load(points, pts_v, 4),
        load(top_t.at[pl.ds(x * 8, 8)], t5_v, 5),
        load(top_t.at[pl.ds(32 + x * 4, 4)], t6_v, 6),
        load(top_t.at[pl.ds(48 + x * 2, 2)], t7_v, 7),
        load(top_t.at[pl.ds(56, 4)], t8_v, 8),
        load(top_c.at[chip], c_v.at[0], 9),
        load(top_c.at[32 + chip // 2], c_v.at[1], 10),
        load(top_c.at[48 + chip // 4], c_v.at[2], 11),
        load(top_c.at[56 + x], c_v.at[3], 12),
        load(top_c.at[60 + x // 2], c_v.at[4], 13),
        load(top_c.at[62], c_v.at[5], 14),
        load(coup, cp_v, 15),
    ]

    barrier = pltpu.get_barrier_semaphore()
    peers = [partner] + zpeers + xpeers
    for peer in peers:
        pl.semaphore_signal(barrier, inc=1, device_id=peer, device_id_type=MESH)

    def span(leaf):
        return pl.ds(leaf * LEAF, LEAF)

    slot = lax.broadcasted_iota(jnp.int32, (LEAF, LEAF), 0)
    order_cp.wait()
    for leaf in range(LEAVES):
        where = ord_v[span(leaf)] & (LEAF - 1)
        pick_v[leaf] = jnp.where(slot == where[None, :], 1.0, 0.0).astype(BF)
    basis_cp.wait()
    for leaf in range(LEAVES):
        bs_v[leaf] = nn(pick_v[leaf], bas_v[leaf]).astype(BF)
    charges_cp.wait()

    def put(node, u):
        uhi[node], ulo[node] = split(u)

    def parent(left, right, mats):
        mats = mats.reshape(2 * RANK, RANK)
        return nn(beside(left[0], right[0]), mats) + nn(beside(left[1], right[1]), mats)

    for leaf in range(LEAVES):
        put(leaf, tn(q_v[span(leaf)], bs_v[leaf]))
    trans_cp.wait()

    def read(node):
        return uhi[node], ulo[node]

    for start, count in ((0, 16), (16, 8), (24, 4)):
        for i in range(count // 2):
            low = start + 2 * i
            put(start + count + i, parent(read(low), read(low + 1), tr_v[low : low + 2]))
    u4_v[...] = parent(read(28), read(29), tr_v[28:30])

    with jax.named_scope("entry"):
        pl.semaphore_wait(barrier, len(peers))
    mine_rows = pl.ds(pl.multiple_of(core * HALF, HALF), HALF)
    other_rows = pl.ds(pl.multiple_of((1 - core) * HALF, HALF), HALF)

    def remote(src, dst, send, recv, peer):
        return pltpu.make_async_remote_copy(
            src_ref=src, dst_ref=dst, send_sem=send, recv_sem=recv, device_id=peer, device_id_type=MESH
        )

    swaps = [
        remote(u4_v.at[other_rows], u4p_v.at[other_rows], cs_s.at[0], cs_r.at[0], partner),
        remote(tr_v.at[30], rp_v, cs_s.at[1], cs_r.at[1], partner),
        remote(u4_v.at[mine_rows], u4p_v.at[mine_rows], cs_s.at[2], cs_r.at[2], partner),
    ]
    for cp in swaps:
        cp.start()
    for cp in late:
        cp.wait()

    t67 = [split(nn(t6_v[i], t7_v[i // 2])) for i in range(4)]
    for i in range(NZ):
        hi, lo = split(mat_times(t5_v[i], t67[i // 2]))
        q2_v[i * RANK : (i + 1) * RANK, :] = beside(hi, lo)
    swaps[0].wait_recv()
    swaps[1].wait_recv()
    u5 = nn(beside(*split(u4_v[mine_rows]), *split(u4p_v[mine_rows])), stacked(tr_v[30], tr_v[30], rp_v[...], rp_v[...]))
    zbuf[z] = u5.astype(BF)
    zsends = [remote(zbuf.at[z], zbuf.at[z], zs.at[k], zr.at[k], zpeers[k]) for k in range(NZ - 1)]
    for k in (3, 2, 4, 1, 5, 0, 6):
        zsends[k].start()

    xs_all = pts_v[...] * SCALE
    h = xs_all.astype(BF).astype(F32)
    rest = xs_all - h
    m = rest.astype(BF).astype(F32)
    low = rest - m
    norm = jnp.sum(xs_all * xs_all, axis=0, keepdims=True)
    nh = norm.astype(BF).astype(F32)
    nrest = norm - nh
    nm = nrest.astype(BF).astype(F32)
    nl = nrest - nm
    wide = norm.shape[1]
    one = jnp.ones((1, wide), F32)
    zero = jnp.zeros((2, wide), F32)
    pad = jnp.zeros((8, wide), F32)
    lhs_v[...] = stacked(h, h, m, m, h, low, nh, nm, nl, one, one, one, zero, pad).astype(BF)
    rhs_v[...] = stacked(2 * h, 2 * m, 2 * h, 2 * m, 2 * low, 2 * h, -one, -one, -one, -nh, -nm, -nl, zero, pad).astype(BF)

    def direct(c, carry):
        spans = [pl.ds(pl.multiple_of((GROUP * c + i) * LEAF, LEAF), LEAF) for i in range(GROUP)]
        for i, where in enumerate(spans):
            e_v[i] = jnp.exp2(tn(lhs_v[:, where], rhs_v[:, where])).astype(BF)
        for i, where in enumerate(spans):
            q = q_v[where]
            out[where, :] = nn(e_v[i], q) + 0.5 * q.astype(F32)
        return carry

    lax.fori_loop(0, LEAVES // GROUP, direct, 0)

    def towards(index, bit):
        mat = c_v[index]
        return jnp.where(bit == 0, mat.astype(F32).T, mat.astype(F32)).astype(BF)

    for i, bit in enumerate((core, z % 2, (z // 2) % 2, z // 4, x % 2, x // 2)):
        m_v[i] = towards(i, bit)

    far = 2 - 2 * (x // 2)
    rest_of_path = nn(m_v[5], t8_v[x].astype(F32).T.astype(BF))
    own_path = pl.ds(pl.multiple_of(z * RANK, RANK), RANK)
    down_path = split(mat_times(tr_v[30], (q2_v[own_path, :RANK], q2_v[own_path, RANK:])))
    from_far = split(rest_of_path)
    down_path = [split(mat_times(tr_v[28 + i], down_path)) for i in range(2)]
    across = [split(mat_times(t8_v[far + i], from_far)) for i in range(2)]
    for i in range(4):
        hi, lo = split(mat_times(tr_v[24 + i], down_path[i // 2]))
        e2_v[i * RANK : (i + 1) * RANK, :] = beside(hi, lo, hi)
    source = stacked(
        beside(m_v[4], m_v[4], jnp.zeros((RANK, RANK), BF)),
        beside(across[0][0], across[0][0], across[0][1]),
        beside(across[1][0], across[1][0], across[1][1]),
    )
    hi, lo = split(nt(source, e2_v[...]))
    h_v[: 3 * RANK] = hi
    h_v[3 * RANK :] = lo

    for pair in range(15):
        mat = cp_v[pair]
        side_v[2 * pair] = times_t(read(2 * pair + 1), mat)
        side_v[2 * pair + 1] = times(read(2 * pair), mat)

    swaps[2].wait_recv()
    side4 = times(split(u4p_v[...]), m_v[0])

    for cp in zsends:
        cp.wait_recv()
    u8 = nn(beside(*[zbuf[i] for i in range(NZ)]), q2_v[...])
    xbuf[x, mine_rows] = (u8[:, :RANK] + u8[:, RANK:]).astype(BF)
    xsends = [
        remote(xbuf.at[x, mine_rows], xbuf.at[x, mine_rows], xs.at[k], xr.at[k], xpeers[k])
        for k in range(2 * (NX - 1))
    ]
    for k in (2, 3, 0, 1, 4, 5):
        xsends[k].start()

    def sibling(i):
        return i + 1 - 2 * (i % 2)

    def level6(i):
        return split(nn(beside(zbuf[2 * i], zbuf[2 * i + 1]), stacked(t5_v[2 * i], t5_v[2 * i + 1])))

    half_z, quarter_z = z // 2, z // 4
    next6 = level6(sibling(half_z))
    other = 1 - quarter_z
    pair6 = level6(2 * other), level6(2 * other + 1)
    side5 = nn(zbuf[sibling(z)], m_v[1])
    side6 = times(next6, m_v[2])
    next7 = split(times(pair6[0], t6_v[2 * other]) + times(pair6[1], t6_v[2 * other + 1]))
    d7 = times(next7, m_v[3])
    d6 = side6 + times_t(split(d7), t6_v[half_z])
    d5_v[mine_rows] = side5 + times_t(split(d6), t5_v[z])
    back = remote(d5_v.at[mine_rows], d5_v.at[mine_rows], ds_s.at[0], ds_r.at[0], partner)
    back.start()
    back.wait_recv()
    d4 = split(side4 + times_t(split(d5_v[...]), tr_v[30]))
    d3 = [split(side_v[28 + i] + times_t(d4, tr_v[28 + i])) for i in range(2)]
    for i in range(4):
        d2_v[i] = side_v[24 + i] + times_t(d3[i // 2], tr_v[24 + i])

    for cp in xsends:
        cp.wait_recv()
    u8s = (xbuf[sibling(x)], xbuf[far], xbuf[far + 1])
    top = nn(beside(*u8s, *u8s), h_v[...])
    d2 = [split(d2_v[i] + top[:, i * RANK : (i + 1) * RANK]) for i in range(4)]
    d1 = [split(side_v[16 + i] + times_t(d2[i // 2], tr_v[16 + i])) for i in range(8)]
    for i in range(LEAVES):
        uhi[i], ulo[i] = split(side_v[i] + times_t(d1[i // 2], tr_v[i]))
    for i in range(LEAVES):
        own = bs_v[i]
        out[span(i), :] += nt(beside(own, own), beside(uhi[i], ulo[i]))

    for cp in swaps + zsends + xsends + [back]:
        cp.wait_send()


def local(*args):
    vm = pltpu.VMEM
    dma = pltpu.SemaphoreType.DMA
    rows = LEAVES * LEAF
    mats = lambda n: vm((n, RANK, RANK), BF)
    return pl.pallas_call(
        kernel,
        out_shape=jax.ShapeDtypeStruct((rows, COLS), F32),
        in_specs=[pl.BlockSpec(memory_space=pltpu.HBM)] * 8,
        out_specs=pl.BlockSpec(memory_space=pltpu.VMEM),
        scratch_shapes=[
            vm((8, rows), F32),
            vm((rows, COLS), BF),
            vm((rows,), jnp.int32),
            vm((LEAVES, LEAF, RANK), BF),
            mats(31),
            mats(15),
            mats(8),
            mats(4),
            mats(2),
            mats(4),
            mats(6),
            vm((LEAVES, LEAF, RANK), BF),
            vm((30, COLS, RANK), BF),
            vm((30, COLS, RANK), BF),
            vm((30, COLS, RANK), F32),
            vm((64, rows), BF),
            vm((64, rows), BF),
            vm((GROUP, LEAF, LEAF), BF),
            vm((LEAVES, LEAF, LEAF), BF),
            vm((COLS, RANK), F32),
            vm((COLS, RANK), F32),
            vm((RANK, RANK), BF),
            vm((NZ, HALF, RANK), BF),
            vm((NX, COLS, RANK), BF),
            vm((COLS, RANK), F32),
            vm((NZ * RANK, 2 * RANK), BF),
            vm((4 * RANK, 3 * RANK), BF),
            vm((6 * RANK, 4 * RANK), BF),
            mats(6),
            vm((4, COLS, RANK), F32),
            dma((16,)),
            dma((3,)),
            dma((3,)),
            dma((NZ - 1,)),
            dma((NZ - 1,)),
            dma((2 * (NX - 1),)),
            dma((2 * (NX - 1),)),
            dma((1,)),
            dma((1,)),
        ],
        compiler_params=pltpu.CompilerParams(
            collective_id=0, has_side_effects=True, vmem_limit_bytes=44 * 1024 * 1024
        ),
    )(*[pltpu.with_memory_space_constraint(arg, pltpu.HBM) for arg in args])


def solution(mesh):
    placed = (
        P(None, "leaf"),
        P("leaf", "rhs"),
        P("leaf"),
        P("leaf", None, None),
        P("leaf", None, None),
        P("leaf", None, None),
        P(),
        P(),
    )
    return jax.shard_map(
        local, mesh=mesh, in_specs=placed, out_specs=P("leaf", "rhs"), check_vma=False
    )
```

time: 43 us -> 23.7 us (0.55)
  Pallas kernels: 31.8 us -> 22.2 us
  local copies, waits for them, and re-layouts: 10.8 us -> 1.32 us
    pallas_call x1, Pallas kernels: 31.8 us -> 22.2 us  [local(): pl.pallas_call(kernel, out_shape=jax.ShapeDtypeStruct((rows, COLS), F32),...]
    unnamed x17 -> x1, local copies, waits for them, and re-layouts: 10.8 us -> 1.32 us
where the time goes in v2:
time: 23.7 us; the launch traced here: 23.6 us
  Pallas kernels  22.2 us (94%)
  local copies, waits for them, and re-layouts  1.32 us (6%)
    pallas_call x1, Pallas kernels, local(): pl.pallas_call(kernel, out_shape=jax.ShapeDtypeStruct((rows, COLS), F32),...  22.2 us
    unnamed x1, local copies, waits for them, and re-layouts  1.32 us

profile of v2, /device:TPU:1, one launch (start us, length us, event | category | flops | bytes accessed | tf_op | source)
XLA Modules:
  0.0 23.6 jit_solution(13197327917060120629)
XLA Ops:
  0.0 22.2 %shard_map.82 = f32[4096,128]{1,0:T(8,128)S(1)} custom-call(f32[8,4096]{1,0:T(8,128)} %points.1, bf16[4096,128]{1,0:T(8,128)(2,1)} %charges.1, s32[4096]{0:T(1024)} %order.1, bf16[16,256,128]{2,1,0:T(8,128)(2,1)} %basis.1, bf16[31,128,128]{2,1,0:T(8,128)(2,1)} %trans.1, bf16[15,128,128]{2,1,0:T(8,128)(2,1)} %coup.1, bf16[62,128,128]{2,1,0:T(8,128)(2,1)} %top_t.1, ...), custom_call_target="tpu_custom_call" | custom-call | tf_op jit(solution)/shard_map/pallas_call | solution.py:290
  22.2 1.3 %copy.10 = f32[4096,128]{1,0:T(8,128)} copy(f32[4096,128]{1,0:T(8,128)S(1)} %shard_map.82) | data formatting | bytes 4194304

commit v3 on v2

--- a/solution.py
+++ b/solution.py
@@ -15,6 +15,7 @@
 NZ, NX = 8, 4
 SCALE = math.sqrt(0.1 * math.log2(math.e))
 GROUP = 8
+PARTS = 8
 
 
 def nn(a, b):
@@ -56,9 +57,9 @@
 
 
 def kernel(
-    points, charges, order, basis, trans, coup, top_t, top_c, out,
+    points, charges, order, basis, trans, coup, top_t, top_c, near, bs_v, dhi, dlo,
     pts_v, q_v, ord_v, bas_v, tr_v, cp_v, t5_v, t6_v, t7_v, t8_v, c_v,
-    bs_v, uhi, ulo, side_v, lhs_v, rhs_v, e_v, pick_v,
+    uhi, ulo, side_v, lhs_v, rhs_v, e_v, pick_v,
     u4_v, u4p_v, rp_v, zbuf, xbuf, d5_v, q2_v, e2_v, h_v, m_v, d2_v,
     in_sem, cs_s, cs_r, zs, zr, xs, xr, ds_s, ds_r,
 ):
@@ -80,27 +81,17 @@
         cp.start()
         return cp
 
+    half = LEAVES // 2
     order_cp = load(order, ord_v, 0)
-    basis_cp = load(basis, bas_v, 1)
-    charges_cp = load(charges, q_v, 2)
-    trans_cp = load(trans, tr_v, 3)
-    late = [
-        load(points, pts_v, 4),
-        load(top_t.at[pl.ds(x * 8, 8)], t5_v, 5),
-        load(top_t.at[pl.ds(32 + x * 4, 4)], t6_v, 6),
-        load(top_t.at[pl.ds(48 + x * 2, 2)], t7_v, 7),
-        load(top_t.at[pl.ds(56, 4)], t8_v, 8),
-        load(top_c.at[chip], c_v.at[0], 9),
-        load(top_c.at[32 + chip // 2], c_v.at[1], 10),
-        load(top_c.at[48 + chip // 4], c_v.at[2], 11),
-        load(top_c.at[56 + x], c_v.at[3], 12),
-        load(top_c.at[60 + x // 2], c_v.at[4], 13),
-        load(top_c.at[62], c_v.at[5], 14),
-        load(coup, cp_v, 15),
-    ]
+    basis_cps, charges_cps = [], []
+    for i in range(2):
+        part, rows = pl.ds(i * half, half), pl.ds(i * half * LEAF, half * LEAF)
+        basis_cps.append(load(basis.at[part], bas_v.at[part], 1 + i))
+        charges_cps.append(load(charges.at[rows], q_v.at[rows], 3 + i))
+    trans_cp = load(trans, tr_v, 5)
 
     barrier = pltpu.get_barrier_semaphore()
-    peers = [partner] + zpeers + xpeers
+    peers = [zpeers[k] for k in (3, 2, 4, 1, 5)] + xpeers + [zpeers[0], zpeers[6], partner]
     for peer in peers:
         pl.semaphore_signal(barrier, inc=1, device_id=peer, device_id_type=MESH)
 
@@ -109,13 +100,6 @@
 
     slot = lax.broadcasted_iota(jnp.int32, (LEAF, LEAF), 0)
     order_cp.wait()
-    for leaf in range(LEAVES):
-        where = ord_v[span(leaf)] & (LEAF - 1)
-        pick_v[leaf] = jnp.where(slot == where[None, :], 1.0, 0.0).astype(BF)
-    basis_cp.wait()
-    for leaf in range(LEAVES):
-        bs_v[leaf] = nn(pick_v[leaf], bas_v[leaf]).astype(BF)
-    charges_cp.wait()
 
     def put(node, u):
         uhi[node], ulo[node] = split(u)
@@ -124,9 +108,33 @@
         mats = mats.reshape(2 * RANK, RANK)
         return nn(beside(left[0], right[0]), mats) + nn(beside(left[1], right[1]), mats)
 
-    for leaf in range(LEAVES):
-        put(leaf, tn(q_v[span(leaf)], bs_v[leaf]))
+    late = []
+    for part in range(2):
+        leaves = range(part * half, (part + 1) * half)
+        for leaf in leaves:
+            where = ord_v[span(leaf)] & (LEAF - 1)
+            pick_v[leaf] = jnp.where(slot == where[None, :], 1.0, 0.0).astype(BF)
+        basis_cps[part].wait()
+        for leaf in leaves:
+            bs_v[leaf] = nn(pick_v[leaf], bas_v[leaf]).astype(BF)
+        charges_cps[part].wait()
+        for leaf in leaves:
+            put(leaf, tn(q_v[span(leaf)], bs_v[leaf]))
     trans_cp.wait()
+    late = [
+        load(top_t.at[pl.ds(x * 8, 8)], t5_v, 6),
+        load(top_t.at[pl.ds(32 + x * 4, 4)], t6_v, 7),
+        load(top_t.at[pl.ds(48 + x * 2, 2)], t7_v, 8),
+        load(top_t.at[pl.ds(56, 4)], t8_v, 9),
+        load(points, pts_v, 10),
+        load(top_c.at[chip], c_v.at[0], 11),
+        load(top_c.at[32 + chip // 2], c_v.at[1], 12),
+        load(top_c.at[48 + chip // 4], c_v.at[2], 13),
+        load(top_c.at[56 + x], c_v.at[3], 14),
+        load(top_c.at[60 + x // 2], c_v.at[4], 15),
+        load(top_c.at[62], c_v.at[5], 16),
+        load(coup, cp_v, 17),
+    ]
 
     def read(node):
         return uhi[node], ulo[node]
@@ -192,7 +200,7 @@
             e_v[i] = jnp.exp2(tn(lhs_v[:, where], rhs_v[:, where])).astype(BF)
         for i, where in enumerate(spans):
             q = q_v[where]
-            out[where, :] = nn(e_v[i], q) + 0.5 * q.astype(F32)
+            near[where, :] = nn(e_v[i], q) + 0.5 * q.astype(F32)
         return carry
 
     lax.fori_loop(0, LEAVES // GROUP, direct, 0)
@@ -273,13 +281,25 @@
     d2 = [split(d2_v[i] + top[:, i * RANK : (i + 1) * RANK]) for i in range(4)]
     d1 = [split(side_v[16 + i] + times_t(d2[i // 2], tr_v[16 + i])) for i in range(8)]
     for i in range(LEAVES):
-        uhi[i], ulo[i] = split(side_v[i] + times_t(d1[i // 2], tr_v[i]))
-    for i in range(LEAVES):
-        own = bs_v[i]
-        out[span(i), :] += nt(beside(own, own), beside(uhi[i], ulo[i]))
+        dhi[i], dlo[i] = split(side_v[i] + times_t(d1[i // 2], tr_v[i]))
 
     for cp in swaps + zsends + xsends + [back]:
         cp.wait_send()
+
+
+def finish(near, bs_v, dhi, dlo, out, sum_v, sem):
+    copies = []
+    for part in range(PARTS):
+        count = LEAVES // PARTS
+        for i in range(part * count, (part + 1) * count):
+            where = pl.ds(i * LEAF, LEAF)
+            own = bs_v[i]
+            sum_v[where] = near[where] + nt(beside(own, own), beside(dhi[i], dlo[i]))
+        where = pl.ds(part * count * LEAF, count * LEAF)
+        copies.append(pltpu.make_async_copy(sum_v.at[where], out.at[where], sem.at[part]))
+        copies[-1].start()
+    for cp in copies:
+        cp.wait()
 
 
 def local(*args):
@@ -287,11 +307,11 @@
     dma = pltpu.SemaphoreType.DMA
     rows = LEAVES * LEAF
     mats = lambda n: vm((n, RANK, RANK), BF)
-    return pl.pallas_call(
+    parts = pl.pallas_call(
         kernel,
-        out_shape=jax.ShapeDtypeStruct((rows, COLS), F32),
+        out_shape=(vm((rows, COLS), F32), vm((LEAVES, LEAF, RANK), BF), mats(LEAVES), mats(LEAVES)),
         in_specs=[pl.BlockSpec(memory_space=pltpu.HBM)] * 8,
-        out_specs=pl.BlockSpec(memory_space=pltpu.VMEM),
+        out_specs=[pl.BlockSpec(memory_space=vm)] * 4,
         scratch_shapes=[
             vm((8, rows), F32),
             vm((rows, COLS), BF),
@@ -304,7 +324,6 @@
             mats(2),
             mats(4),
             mats(6),
-            vm((LEAVES, LEAF, RANK), BF),
             vm((30, COLS, RANK), BF),
             vm((30, COLS, RANK), BF),
             vm((30, COLS, RANK), F32),
@@ -323,7 +342,7 @@
             vm((6 * RANK, 4 * RANK), BF),
             mats(6),
             vm((4, COLS, RANK), F32),
-            dma((16,)),
+            dma((18,)),
             dma((3,)),
             dma((3,)),
             dma((NZ - 1,)),
@@ -337,6 +356,14 @@
             collective_id=0, has_side_effects=True, vmem_limit_bytes=44 * 1024 * 1024
         ),
     )(*[pltpu.with_memory_space_constraint(arg, pltpu.HBM) for arg in args])
+    return pl.pallas_call(
+        finish,
+        out_shape=jax.ShapeDtypeStruct((rows, COLS), F32),
+        in_specs=[pl.BlockSpec(memory_space=vm)] * 4,
+        out_specs=pl.BlockSpec(memory_space=pltpu.HBM),
+        scratch_shapes=[vm((rows, COLS), F32), dma((PARTS,))],
+        compiler_params=pltpu.CompilerParams(vmem_limit_bytes=16 * 1024 * 1024),
+    )(*[pltpu.with_memory_space_constraint(part, vm) for part in parts])
 
 
 def solution(mesh):

time: 23.7 us -> 24.2 us (1.021)
  Pallas kernels: 22.2 us -> 24 us
  local copies, waits for them, and re-layouts: 1.32 us -> 0 us
    pallas_call x1 -> x2, Pallas kernels: 22.2 us -> 24 us  [the longest x1 22.4 us: local(): pl.pallas_call(kernel, out_shape=(vm((rows, COLS), F32), vm((LEAVES, LEAF...]
    unnamed x1 -> x0, local copies, waits for them, and re-layouts: 1.32 us -> none
where the time goes in v3:
time: 24.2 us; the launch traced here: 24 us
  Pallas kernels  24 us (99%)
    pallas_call x1, Pallas kernels, local(): pl.pallas_call(kernel, out_shape=(vm((rows, COLS), F32), vm((LEAVES, LEAF...  22.4 us
    pallas_call x1, Pallas kernels, local(): pl.pallas_call(finish, out_shape=jax.ShapeDtypeStruct((rows, COLS), F32),...  1.61 us

profile of v3, /device:TPU:1, one launch (start us, length us, event | category | flops | bytes accessed | tf_op | source)
XLA Modules:
  0.0 24.0 jit_solution(13123183150976343113)
XLA Ops:
  0.0 22.4 %shard_map.82 = (f32[4096,128]{1,0:T(8,128)S(1)}, bf16[16,256,128]{2,1,0:T(8,128)(2,1)S(1)}, bf16[16,128,128]{2,1,0:T(8,128)(2,1)S(1)}, bf16[16,128,128]{2,1,0:T(8,128)(2,1)S(1)}) custom-call(f32[8,4096]{1,0:T(8,128)} %points.1, bf16[4096,128]{1,0:T(8,128)(2,1)} %charges.1, s32[4096]{0:T(1024)} %order.1, bf16[16,256,128]{2,1,0:T(8,128)(2,1)} %basis.1, ...), custom_call_target="tpu_custom_call" | custom-call | tf_op jit(solution)/shard_map/pallas_call | solution.py:310
  22.4 1.6 %shard_map.83 = f32[4096,128]{1,0:T(8,128)} custom-call(f32[4096,128]{1,0:T(8,128)S(1)} %get-tuple-element.9.near, bf16[16,256,128]{2,1,0:T(8,128)(2,1)S(1)} %get-tuple-element.10.bs_v, bf16[16,128,128]{2,1,0:T(8,128)(2,1)S(1)} %get-tuple-element.11.dhi, bf16[16,128,128]{2,1,0:T(8,128)(2,1)S(1)} %get-tuple-element.12.dlo), custom_call_target="tpu_custom_call" | custom-call | tf_op jit(solution)/shard_map/pallas_call | solution.py:359

commit v4 on v3

v4 whole, which is shorter than its diff:
```python
import functools
import math

import jax
import jax.numpy as jnp
from jax import lax
from jax.experimental import pallas as pl
from jax.experimental.pallas import tpu as pltpu
from jax.sharding import PartitionSpec as P

MESH = pl.DeviceIdType.MESH
BF, F32 = jnp.bfloat16, jnp.float32
LEAF, RANK, COLS, LEAVES = 256, 128, 128, 16
HALF = COLS // 2
NZ, NX = 8, 4
SCALE = math.sqrt(0.1 * math.log2(math.e))
GROUP = 4
PARTS = 8


def nn(a, b):
    return lax.dot_general(a, b, (((1,), (0,)), ((), ())), preferred_element_type=F32)


def nt(a, b):
    return lax.dot_general(a, b, (((1,), (1,)), ((), ())), preferred_element_type=F32)


def tn(a, b):
    return lax.dot_general(a, b, (((0,), (0,)), ((), ())), preferred_element_type=F32)


def split(u):
    hi = u.astype(BF)
    return hi, (u - hi.astype(F32)).astype(BF)


def beside(*parts):
    return jnp.concatenate(parts, axis=1)


def stacked(*parts):
    return jnp.concatenate(parts, axis=0)


def times(u, mat):
    return nn(beside(*u), stacked(mat, mat))


def times_t(u, mat):
    return nt(beside(*u), beside(mat, mat))


def mat_times(mat, u):
    both = nn(mat, beside(*u))
    return both[:, :RANK] + both[:, RANK:]


def kernel(
    points, charges, order, basis, trans, coup, top_t, top_c, near, bs_v, dhi, dlo,
    pts_v, q_v, ord_v, bas_v, tr_v, cp_v, t5_v, t6_v, t7_v, t8_v, c_v,
    uhi, ulo, side_v, lhs_v, rhs_v, e_v, pick_v,
    p_v, pp_v, u4_v, u4p_v, zbuf, xbuf, d5_v, g_v, q2_v, e0_v, src_v, h_v, m_v, d0_v,
    in_sem, cs_s, cs_r, zs, zr, xs, xr, ds_s, ds_r,
):
    me, col = lax.axis_index("leaf"), lax.axis_index("rhs")
    core = me % 2
    z = (me // 2) % NZ
    x = me // (2 * NZ)
    chip = me // 2

    def at(xx, zz, cc):
        return ((xx * NZ + zz) * 2 + cc, col)

    partner = at(x, z, 1 - core)
    zpeers = [at(x, (z + k) % NZ, core) for k in range(1, NZ)]
    xpeers = [at((x + k) % NX, z, cc) for k in range(1, NX) for cc in (core, 1 - core)]

    def load(src, dst, sem):
        cp = pltpu.make_async_copy(src, dst, in_sem.at[sem])
        cp.start()
        return cp

    order_cp = load(order, ord_v, 0)
    basis_cp = load(basis, bas_v, 1)
    charges_cp = load(charges, q_v, 2)
    trans_cp = load(trans, tr_v, 3)

    barrier = pltpu.get_barrier_semaphore()
    peers = [zpeers[k] for k in (3, 2, 4, 1, 5)] + xpeers + [zpeers[0], zpeers[6], partner]
    for peer in peers:
        pl.semaphore_signal(barrier, inc=1, device_id=peer, device_id_type=MESH)

    def span(leaf):
        return pl.ds(leaf * LEAF, LEAF)

    slot = lax.broadcasted_iota(jnp.int32, (LEAF, LEAF), 0)
    order_cp.wait()
    for leaf in range(LEAVES):
        where = ord_v[span(leaf)] & (LEAF - 1)
        pick_v[leaf] = jnp.where(slot == where[None, :], 1.0, 0.0).astype(BF)
    basis_cp.wait()
    for leaf in range(LEAVES):
        bs_v[leaf] = nn(pick_v[leaf], bas_v[leaf]).astype(BF)
    charges_cp.wait()

    def put(node, u):
        uhi[node], ulo[node] = split(u)

    def read(node):
        return uhi[node], ulo[node]

    def parent(left, right, mats):
        mats = mats.reshape(2 * RANK, RANK)
        return nn(beside(left[0], right[0]), mats) + nn(beside(left[1], right[1]), mats)

    def raise_level(start, count):
        for i in range(count // 2):
            low = start + 2 * i
            put(start + count + i, parent(read(low), read(low + 1), tr_v[low : low + 2]))

    for leaf in range(LEAVES):
        put(leaf, tn(q_v[span(leaf)], bs_v[leaf]))
    trans_cp.wait()
    late = [
        load(points, pts_v, 4),
        load(top_t.at[pl.ds(x * 8, 8)], t5_v, 5),
        load(top_t.at[pl.ds(32 + x * 4, 4)], t6_v, 6),
        load(top_t.at[pl.ds(48 + x * 2, 2)], t7_v, 7),
        load(top_t.at[pl.ds(56, 4)], t8_v, 8),
        load(top_c.at[chip], c_v.at[0], 9),
        load(top_c.at[32 + chip // 2], c_v.at[1], 10),
        load(top_c.at[48 + chip // 4], c_v.at[2], 11),
        load(top_c.at[56 + x], c_v.at[3], 12),
        load(top_c.at[60 + x // 2], c_v.at[4], 13),
        load(top_c.at[62], c_v.at[5], 14),
        load(coup, cp_v, 15),
    ]

    root = tr_v[30]
    paths = [split(nn(tr_v[28 + i], root)) for i in range(2)]
    raise_level(0, 16)
    for i in range(4):
        hi, lo = split(mat_times(tr_v[24 + i], paths[i // 2]))
        for j, part in enumerate((hi, lo, hi)):
            g_v[(4 * j + i) * RANK : (4 * j + i + 1) * RANK, :] = part
    raise_level(16, 8)
    highs = [uhi[24 + i] for i in range(4)]
    p_v[...] = nn(beside(*highs, *highs, *[ulo[24 + i] for i in range(4)]), g_v[...])

    pl.semaphore_wait(barrier, len(peers))
    mine_rows = pl.ds(pl.multiple_of(core * HALF, HALF), HALF)
    other_rows = pl.ds(pl.multiple_of((1 - core) * HALF, HALF), HALF)

    def remote(src, dst, send, recv, peer):
        return pltpu.make_async_remote_copy(
            src_ref=src, dst_ref=dst, send_sem=send, recv_sem=recv, device_id=peer, device_id_type=MESH
        )

    swap = remote(p_v.at[other_rows], pp_v, cs_s.at[0], cs_r.at[0], partner)
    swap.start()
    swap.wait_recv()
    zbuf[z] = (p_v[mine_rows] + pp_v[...]).astype(BF)
    zsends = [remote(zbuf.at[z], zbuf.at[z], zs.at[k], zr.at[k], zpeers[k]) for k in range(NZ - 1)]
    for k in (3, 2, 4, 1, 5, 0, 6):
        zsends[k].start()

    raise_level(24, 4)
    u4_v[...] = parent(read(28), read(29), tr_v[28:30])
    swap4 = remote(u4_v, u4p_v, cs_s.at[1], cs_r.at[1], partner)
    swap4.start()
    for cp in late:
        cp.wait()

    t67 = [split(nn(t6_v[i], t7_v[i // 2])) for i in range(4)]

    xs_all = pts_v[...] * SCALE
    h = xs_all.astype(BF).astype(F32)
    rest = xs_all - h
    m = rest.astype(BF).astype(F32)
    low = rest - m
    norm = jnp.sum(xs_all * xs_all, axis=0, keepdims=True)
    nh = norm.astype(BF).astype(F32)
    nrest = norm - nh
    nm = nrest.astype(BF).astype(F32)
    nl = nrest - nm
    wide = norm.shape[1]
    one = jnp.ones((1, wide), F32)
    zero = jnp.zeros((2, wide), F32)
    pad = jnp.zeros((8, wide), F32)
    lhs_v[...] = stacked(h, h, m, m, h, low, nh, nm, nl, one, one, one, zero, pad).astype(BF)
    rhs_v[...] = stacked(2 * h, 2 * m, 2 * h, 2 * m, 2 * low, 2 * h, -one, -one, -one, -nh, -nm, -nl, zero, pad).astype(BF)

    for i in range(NZ):
        hi, lo = split(mat_times(t5_v[i], t67[i // 2]))
        q2_v[i * RANK : (i + 1) * RANK, :] = beside(hi, lo)

    def towards(index, bit):
        mat = c_v[index]
        return jnp.where(bit == 0, mat.astype(F32).T, mat.astype(F32)).astype(BF)

    for i, bit in enumerate((core, z % 2, (z // 2) % 2, z // 4, x % 2, x // 2)):
        m_v[i] = towards(i, bit)

    def blocks(leaves):
        for leaf in leaves:
            where = span(leaf)
            e_v[leaf % (2 * GROUP)] = jnp.exp2(tn(lhs_v[:, where], rhs_v[:, where])).astype(BF)

    def direct(leaves):
        for leaf in leaves:
            q = q_v[span(leaf)]
            near[span(leaf), :] = nn(e_v[leaf % (2 * GROUP)], q) + 0.5 * q.astype(F32)

    far = 2 - 2 * (x // 2)
    own_path = pl.ds(pl.multiple_of(z * RANK, RANK), RANK)
    blocks(range(GROUP))
    down_path = [split(mat_times(root, (q2_v[own_path, :RANK], q2_v[own_path, RANK:])))]
    from_far = split(nn(m_v[5], t8_v[x].astype(F32).T.astype(BF)))
    across = []
    for group, start in ((0, 28), (1, 24), (2, 16), (3, 0)):
        if group < 3:
            blocks(range((group + 1) * GROUP, (group + 2) * GROUP))
        count = 2 * len(down_path)
        down_path = [split(mat_times(tr_v[start + i], down_path[i // 2])) for i in range(count)]
        if group == 0:
            across = [split(mat_times(t8_v[far + i], from_far)) for i in range(2)]
        direct(range(group * GROUP, (group + 1) * GROUP))
    for i in range(LEAVES):
        hi, lo = down_path[i]
        e0_v[i * RANK : (i + 1) * RANK, :] = beside(hi, lo, hi)
    src_v[...] = stacked(
        beside(m_v[4], m_v[4], jnp.zeros((RANK, RANK), BF)),
        beside(across[0][0], across[0][0], across[0][1]),
        beside(across[1][0], across[1][0], across[1][1]),
    )
    for pair in range(15):
        mat = cp_v[pair]
        side_v[2 * pair] = times_t(read(2 * pair + 1), mat)
        side_v[2 * pair + 1] = times(read(2 * pair), mat)

    for cp in zsends:
        cp.wait_recv()
    u8 = nn(beside(*[zbuf[i] for i in range(NZ)]), q2_v[...])
    xbuf[x, mine_rows] = (u8[:, :RANK] + u8[:, RANK:]).astype(BF)
    xsends = [
        remote(xbuf.at[x, mine_rows], xbuf.at[x, mine_rows], xs.at[k], xr.at[k], xpeers[k])
        for k in range(2 * (NX - 1))
    ]
    for k in (2, 3, 0, 1, 4, 5):
        xsends[k].start()

    def sibling(i):
        return i + 1 - 2 * (i % 2)

    def level6(i):
        return split(nn(beside(zbuf[2 * i], zbuf[2 * i + 1]), stacked(t5_v[2 * i], t5_v[2 * i + 1])))

    half_z, quarter_z = z // 2, z // 4
    other = 1 - quarter_z
    next6, pair6 = level6(sibling(half_z)), (level6(2 * other), level6(2 * other + 1))
    side5 = nn(zbuf[sibling(z)], m_v[1])
    next7 = split(times(pair6[0], t6_v[2 * other]) + times(pair6[1], t6_v[2 * other + 1]))
    side6 = times(next6, m_v[2])
    d7 = times(next7, m_v[3])
    d6 = side6 + times_t(split(d7), t6_v[half_z])
    d5_v[mine_rows] = side5 + times_t(split(d6), t5_v[z])
    back = remote(d5_v.at[mine_rows], d5_v.at[mine_rows], ds_s.at[0], ds_r.at[0], partner)
    back.start()
    for i in range(LEAVES // 2):
        where = slice(2 * i * RANK, 2 * (i + 1) * RANK)
        hi, lo = split(nt(src_v[...], e0_v[where]))
        h_v[: 3 * RANK, where] = hi
        h_v[3 * RANK :, where] = lo
    swap4.wait_recv()
    side4 = times(split(u4p_v[...]), m_v[0])
    back.wait_recv()
    down = [split(side4 + times_t(split(d5_v[...]), root))]
    for start, count in ((28, 2), (24, 4), (16, 8)):
        down = [split(side_v[start + i] + times_t(down[i // 2], tr_v[start + i])) for i in range(count)]
    for i in range(LEAVES):
        d0_v[i] = side_v[i] + times_t(down[i // 2], tr_v[i])

    for cp in xsends:
        cp.wait_recv()
    u8s = (xbuf[sibling(x)], xbuf[far], xbuf[far + 1])
    u8s = beside(*u8s, *u8s)
    for i in range(LEAVES // 2):
        top = nn(u8s, h_v[:, 2 * i * RANK : 2 * (i + 1) * RANK])
        for j in range(2):
            leaf = 2 * i + j
            dhi[leaf], dlo[leaf] = split(d0_v[leaf] + top[:, j * RANK : (j + 1) * RANK])

    for cp in [swap, swap4] + zsends + xsends + [back]:
        cp.wait_send()


def finish(near, bs_v, dhi, dlo, out, sum_v, sem):
    copies = []
    for part in range(PARTS):
        count = LEAVES // PARTS
        for i in range(part * count, (part + 1) * count):
            where = pl.ds(i * LEAF, LEAF)
            own = bs_v[i]
            sum_v[where] = near[where] + nt(beside(own, own), beside(dhi[i], dlo[i]))
        where = pl.ds(part * count * LEAF, count * LEAF)
        copies.append(pltpu.make_async_copy(sum_v.at[where], out.at[where], sem.at[part]))
        copies[-1].start()
    for cp in copies:
        cp.wait()


def local(*args):
    vm = pltpu.VMEM
    dma = pltpu.SemaphoreType.DMA
    rows = LEAVES * LEAF
    mats = lambda n: vm((n, RANK, RANK), BF)
    parts = pl.pallas_call(
        kernel,
        out_shape=(vm((rows, COLS), F32), vm((LEAVES, LEAF, RANK), BF), mats(LEAVES), mats(LEAVES)),
        in_specs=[pl.BlockSpec(memory_space=pltpu.HBM)] * 8,
        out_specs=[pl.BlockSpec(memory_space=vm)] * 4,
        scratch_shapes=[
            vm((8, rows), F32),
            vm((rows, COLS), BF),
            vm((rows,), jnp.int32),
            vm((LEAVES, LEAF, RANK), BF),
            mats(31),
            mats(15),
            mats(8),
            mats(4),
            mats(2),
            mats(4),
            mats(6),
            vm((30, COLS, RANK), BF),
            vm((30, COLS, RANK), BF),
            vm((30, COLS, RANK), F32),
            vm((64, rows), BF),
            vm((64, rows), BF),
            vm((2 * GROUP, LEAF, LEAF), BF),
            vm((LEAVES, LEAF, LEAF), BF),
            vm((COLS, RANK), F32),
            vm((HALF, RANK), F32),
            vm((COLS, RANK), F32),
            vm((COLS, RANK), F32),
            vm((NZ, HALF, RANK), BF),
            vm((NX, COLS, RANK), BF),
            vm((COLS, RANK), F32),
            vm((12 * RANK, RANK), BF),
            vm((NZ * RANK, 2 * RANK), BF),
            vm((LEAVES * RANK, 3 * RANK), BF),
            vm((3 * RANK, 3 * RANK), BF),
            vm((6 * RANK, LEAVES * RANK), BF),
            mats(6),
            vm((LEAVES, COLS, RANK), F32),
            dma((16,)),
            dma((2,)),
            dma((2,)),
            dma((NZ - 1,)),
            dma((NZ - 1,)),
            dma((2 * (NX - 1),)),
            dma((2 * (NX - 1),)),
            dma((1,)),
            dma((1,)),
        ],
        compiler_params=pltpu.CompilerParams(
            collective_id=0, has_side_effects=True, vmem_limit_bytes=44 * 1024 * 1024
        ),
    )(*[pltpu.with_memory_space_constraint(arg, pltpu.HBM) for arg in args])
    return pl.pallas_call(
        finish,
        out_shape=jax.ShapeDtypeStruct((rows, COLS), F32),
        in_specs=[pl.BlockSpec(memory_space=vm)] * 4,
        out_specs=pl.BlockSpec(memory_space=pltpu.HBM),
        scratch_shapes=[vm((rows, COLS), F32), dma((PARTS,))],
        compiler_params=pltpu.CompilerParams(vmem_limit_bytes=16 * 1024 * 1024),
    )(*[pltpu.with_memory_space_constraint(part, vm) for part in parts])


def solution(mesh):
    placed = (
        P(None, "leaf"),
        P("leaf", "rhs"),
        P("leaf"),
        P("leaf", None, None),
        P("leaf", None, None),
        P("leaf", None, None),
        P(),
        P(),
    )
    return jax.shard_map(
        local, mesh=mesh, in_specs=placed, out_specs=P("leaf", "rhs"), check_vma=False
    )
```

time: 24.2 us -> 23.1 us (0.955)
  Pallas kernels: 24 us -> 22.9 us
    pallas_call x1, Pallas kernels: 22.4 us -> 21.3 us  [local(): pl.pallas_call(kernel, out_shape=(vm((rows, COLS), F32), vm((LEAVES, LEAF...]
where the time goes in v4:
time: 23.1 us; the launch traced here: 23 us
  Pallas kernels  22.9 us (99%)
    pallas_call x1, Pallas kernels, local(): pl.pallas_call(kernel, out_shape=(vm((rows, COLS), F32), vm((LEAVES, LEAF...  21.3 us
    pallas_call x1, Pallas kernels, local(): pl.pallas_call(finish, out_shape=jax.ShapeDtypeStruct((rows, COLS), F32),...  1.61 us

profile of v4, /device:TPU:1, one launch (start us, length us, event | category | flops | bytes accessed | tf_op | source)
XLA Modules:
  0.0 23.0 jit_solution(17897351077371661181)
XLA Ops:
  0.0 21.3 %shard_map.82 = (f32[4096,128]{1,0:T(8,128)S(1)}, bf16[16,256,128]{2,1,0:T(8,128)(2,1)S(1)}, bf16[16,128,128]{2,1,0:T(8,128)(2,1)S(1)}, bf16[16,128,128]{2,1,0:T(8,128)(2,1)S(1)}) custom-call(f32[8,4096]{1,0:T(8,128)} %points.1, bf16[4096,128]{1,0:T(8,128)(2,1)} %charges.1, s32[4096]{0:T(1024)} %order.1, bf16[16,256,128]{2,1,0:T(8,128)(2,1)} %basis.1, ...), custom_call_target="tpu_custom_call" | custom-call | tf_op jit(solution)/shard_map/pallas_call | solution.py:318
  21.3 1.6 %shard_map.83 = f32[4096,128]{1,0:T(8,128)} custom-call(f32[4096,128]{1,0:T(8,128)S(1)} %get-tuple-element.9.near, bf16[16,256,128]{2,1,0:T(8,128)(2,1)S(1)} %get-tuple-element.10.bs_v, bf16[16,128,128]{2,1,0:T(8,128)(2,1)S(1)} %get-tuple-element.11.dhi, bf16[16,128,128]{2,1,0:T(8,128)(2,1)S(1)} %get-tuple-element.12.dlo), custom_call_target="tpu_custom_call" | custom-call | tf_op jit(solution)/shard_map/pallas_call | solution.py:370

commit v5 on v4

--- a/solution.py
+++ b/solution.py
@@ -15,7 +15,6 @@
 NZ, NX = 8, 4
 SCALE = math.sqrt(0.1 * math.log2(math.e))
 GROUP = 4
-PARTS = 8
 
 
 def nn(a, b):
@@ -57,10 +56,10 @@
 
 
 def kernel(
-    points, charges, order, basis, trans, coup, top_t, top_c, near, bs_v, dhi, dlo,
+    points, charges, order, basis, trans, coup, top_t, top_c, near, bs_v, d0_v, h_v, ups,
     pts_v, q_v, ord_v, bas_v, tr_v, cp_v, t5_v, t6_v, t7_v, t8_v, c_v,
     uhi, ulo, side_v, lhs_v, rhs_v, e_v, pick_v,
-    p_v, pp_v, u4_v, u4p_v, zbuf, xbuf, d5_v, g_v, q2_v, e0_v, src_v, h_v, m_v, d0_v,
+    p_v, pp_v, u4_v, u4p_v, zbuf, xbuf, d5_v, g_v, q2_v, e0_v, src_v, m_v, qp_v,
     in_sem, cs_s, cs_r, zs, zr, xs, xr, ds_s, ds_r,
 ):
     me, col = lax.axis_index("leaf"), lax.axis_index("rhs")
@@ -82,8 +81,8 @@
         return cp
 
     order_cp = load(order, ord_v, 0)
-    basis_cp = load(basis, bas_v, 1)
-    charges_cp = load(charges, q_v, 2)
+    charges_cp = load(charges, q_v, 1)
+    basis_cp = load(basis, bas_v, 2)
     trans_cp = load(trans, tr_v, 3)
 
     barrier = pltpu.get_barrier_semaphore()
@@ -99,10 +98,10 @@
     for leaf in range(LEAVES):
         where = ord_v[span(leaf)] & (LEAF - 1)
         pick_v[leaf] = jnp.where(slot == where[None, :], 1.0, 0.0).astype(BF)
+    charges_cp.wait()
+    for leaf in range(LEAVES):
+        qp_v[leaf] = tn(q_v[span(leaf)], pick_v[leaf]).astype(BF)
     basis_cp.wait()
-    for leaf in range(LEAVES):
-        bs_v[leaf] = nn(pick_v[leaf], bas_v[leaf]).astype(BF)
-    charges_cp.wait()
 
     def put(node, u):
         uhi[node], ulo[node] = split(u)
@@ -120,7 +119,7 @@
             put(start + count + i, parent(read(low), read(low + 1), tr_v[low : low + 2]))
 
     for leaf in range(LEAVES):
-        put(leaf, tn(q_v[span(leaf)], bs_v[leaf]))
+        put(leaf, nn(qp_v[leaf], bas_v[leaf]))
     trans_cp.wait()
     late = [
         load(points, pts_v, 4),
@@ -234,6 +233,8 @@
         beside(across[0][0], across[0][0], across[0][1]),
         beside(across[1][0], across[1][0], across[1][1]),
     )
+    for leaf in range(LEAVES):
+        bs_v[leaf] = nn(pick_v[leaf], bas_v[leaf]).astype(BF)
     for pair in range(15):
         mat = cp_v[pair]
         side_v[2 * pair] = times_t(read(2 * pair + 1), mat)
@@ -283,28 +284,32 @@
 
     for cp in xsends:
         cp.wait_recv()
-    u8s = (xbuf[sibling(x)], xbuf[far], xbuf[far + 1])
-    u8s = beside(*u8s, *u8s)
+    ups[...] = beside(xbuf[sibling(x)], xbuf[far], xbuf[far + 1])
+
+    for cp in [swap, swap4] + zsends + xsends + [back]:
+        cp.wait_send()
+
+
+def finish(near, bs_v, d0_v, h_v, ups, out, sum_v, sem):
+    u8s = beside(ups[...], ups[...])
+
+    def top(i):
+        return nn(u8s, h_v[:, 2 * i * RANK : 2 * (i + 1) * RANK])
+
+    copies = []
+    ahead = top(0)
     for i in range(LEAVES // 2):
-        top = nn(u8s, h_v[:, 2 * i * RANK : 2 * (i + 1) * RANK])
+        part = ahead
+        if i + 1 < LEAVES // 2:
+            ahead = top(i + 1)
         for j in range(2):
             leaf = 2 * i + j
-            dhi[leaf], dlo[leaf] = split(d0_v[leaf] + top[:, j * RANK : (j + 1) * RANK])
-
-    for cp in [swap, swap4] + zsends + xsends + [back]:
-        cp.wait_send()
-
-
-def finish(near, bs_v, dhi, dlo, out, sum_v, sem):
-    copies = []
-    for part in range(PARTS):
-        count = LEAVES // PARTS
-        for i in range(part * count, (part + 1) * count):
-            where = pl.ds(i * LEAF, LEAF)
-            own = bs_v[i]
-            sum_v[where] = near[where] + nt(beside(own, own), beside(dhi[i], dlo[i]))
-        where = pl.ds(part * count * LEAF, count * LEAF)
-        copies.append(pltpu.make_async_copy(sum_v.at[where], out.at[where], sem.at[part]))
+            where = pl.ds(leaf * LEAF, LEAF)
+            own = bs_v[leaf]
+            down = split(d0_v[leaf] + part[:, j * RANK : (j + 1) * RANK])
+            sum_v[where] = near[where] + nt(beside(own, own), beside(*down))
+        where = pl.ds(2 * i * LEAF, 2 * LEAF)
+        copies.append(pltpu.make_async_copy(sum_v.at[where], out.at[where], sem.at[i]))
         copies[-1].start()
     for cp in copies:
         cp.wait()
@@ -317,9 +322,15 @@
     mats = lambda n: vm((n, RANK, RANK), BF)
     parts = pl.pallas_call(
         kernel,
-        out_shape=(vm((rows, COLS), F32), vm((LEAVES, LEAF, RANK), BF), mats(LEAVES), mats(LEAVES)),
+        out_shape=(
+            vm((rows, COLS), F32),
+            vm((LEAVES, LEAF, RANK), BF),
+            vm((LEAVES, COLS, RANK), F32),
+            vm((6 * RANK, LEAVES * RANK), BF),
+            vm((COLS, 3 * RANK), BF),
+        ),
         in_specs=[pl.BlockSpec(memory_space=pltpu.HBM)] * 8,
-        out_specs=[pl.BlockSpec(memory_space=vm)] * 4,
+        out_specs=[pl.BlockSpec(memory_space=vm)] * 5,
         scratch_shapes=[
             vm((8, rows), F32),
             vm((rows, COLS), BF),
@@ -350,9 +361,8 @@
             vm((NZ * RANK, 2 * RANK), BF),
             vm((LEAVES * RANK, 3 * RANK), BF),
             vm((3 * RANK, 3 * RANK), BF),
-            vm((6 * RANK, LEAVES * RANK), BF),
             mats(6),
-            vm((LEAVES, COLS, RANK), F32),
+            vm((LEAVES, COLS, LEAF), BF),
             dma((16,)),
             dma((2,)),
             dma((2,)),
@@ -370,9 +380,9 @@
     return pl.pallas_call(
         finish,
         out_shape=jax.ShapeDtypeStruct((rows, COLS), F32),
-        in_specs=[pl.BlockSpec(memory_space=vm)] * 4,
+        in_specs=[pl.BlockSpec(memory_space=vm)] * 5,
         out_specs=pl.BlockSpec(memory_space=pltpu.HBM),
-        scratch_shapes=[vm((rows, COLS), F32), dma((PARTS,))],
+        scratch_shapes=[vm((rows, COLS), F32), dma((LEAVES // 2,))],
         compiler_params=pltpu.CompilerParams(vmem_limit_bytes=16 * 1024 * 1024),
     )(*[pltpu.with_memory_space_constraint(part, vm) for part in parts])
 

time: 23.1 us -> 23 us (level)
    pallas_call x1, Pallas kernels: 21.3 us -> 20.5 us  [local(): pl.pallas_call(kernel, out_shape=(vm((rows, COLS), F32), vm((LEAVES, LEAF...]
    pallas_call x1, Pallas kernels: 1.61 us -> 2.31 us  [local(): pl.pallas_call(finish, out_shape=jax.ShapeDtypeStruct((rows, COLS), F32),...]
where the time goes in v5:
time: 23 us; the launch traced here: 22.8 us
  Pallas kernels  22.8 us (99%)
    pallas_call x1, Pallas kernels, local(): pl.pallas_call(kernel, out_shape=(vm((rows, COLS), F32), vm((LEAVES, LEAF...  20.5 us
    pallas_call x1, Pallas kernels, local(): pl.pallas_call(finish, out_shape=jax.ShapeDtypeStruct((rows, COLS), F32),...  2.31 us

profile of v5, /device:TPU:1, one launch (start us, length us, event | category | flops | bytes accessed | tf_op | source)
XLA Modules:
  0.0 22.8 jit_solution(8020027967119902459)
XLA Ops:
  0.0 20.5 %shard_map.82 = (f32[4096,128]{1,0:T(8,128)S(1)}, bf16[16,256,128]{2,1,0:T(8,128)(2,1)S(1)}, f32[16,128,128]{2,1,0:T(8,128)S(1)}, bf16[768,2048]{1,0:T(8,128)(2,1)S(1)}, bf16[128,384]{1,0:T(8,128)(2,1)S(1)}) custom-call(f32[8,4096]{1,0:T(8,128)} %points.1, bf16[4096,128]{1,0:T(8,128)(2,1)} %charges.1, s32[4096]{0:T(1024)} %order.1, ...), custom_call_target="tpu_custom_call" | custom-call | tf_op jit(solution)/shard_map/pallas_call | solution.py:323
  20.5 2.3 %shard_map.83 = f32[4096,128]{1,0:T(8,128)} custom-call(f32[4096,128]{1,0:T(8,128)S(1)} %get-tuple-element.10.near, bf16[16,256,128]{2,1,0:T(8,128)(2,1)S(1)} %get-tuple-element.11.bs_v, f32[16,128,128]{2,1,0:T(8,128)S(1)} %get-tuple-element.12.d0_v, bf16[768,2048]{1,0:T(8,128)(2,1)S(1)} %get-tuple-element.13.h_v, bf16[128,384]{1,0:T(8,128)(2,1)S(1)} %get-tuple-element.14.ups), custom_call_target="tpu_custom_call" | custom-call | tf_op jit(solution)/shard_map/pallas_call | solution.py:380

commit v6 on v5

--- a/solution.py
+++ b/solution.py
@@ -121,6 +121,29 @@
     for leaf in range(LEAVES):
         put(leaf, nn(qp_v[leaf], bas_v[leaf]))
     trans_cp.wait()
+
+    root = tr_v[30]
+    paths = [split(nn(tr_v[28 + i], root)) for i in range(2)]
+    raise_level(0, 16)
+    for i in range(4):
+        hi, lo = split(mat_times(tr_v[24 + i], paths[i // 2]))
+        for j, part in enumerate((hi, lo, hi)):
+            g_v[(4 * j + i) * RANK : (4 * j + i + 1) * RANK, :] = part
+    raise_level(16, 8)
+    highs = [uhi[24 + i] for i in range(4)]
+    p_v[...] = nn(beside(*highs, *highs, *[ulo[24 + i] for i in range(4)]), g_v[...])
+
+    pl.semaphore_wait(barrier, len(peers))
+    mine_rows = pl.ds(pl.multiple_of(core * HALF, HALF), HALF)
+    other_rows = pl.ds(pl.multiple_of((1 - core) * HALF, HALF), HALF)
+
+    def remote(src, dst, send, recv, peer):
+        return pltpu.make_async_remote_copy(
+            src_ref=src, dst_ref=dst, send_sem=send, recv_sem=recv, device_id=peer, device_id_type=MESH
+        )
+
+    swap = remote(p_v.at[other_rows], pp_v, cs_s.at[0], cs_r.at[0], partner)
+    swap.start()
     late = [
         load(points, pts_v, 4),
         load(top_t.at[pl.ds(x * 8, 8)], t5_v, 5),
@@ -135,29 +158,6 @@
         load(top_c.at[62], c_v.at[5], 14),
         load(coup, cp_v, 15),
     ]
-
-    root = tr_v[30]
-    paths = [split(nn(tr_v[28 + i], root)) for i in range(2)]
-    raise_level(0, 16)
-    for i in range(4):
-        hi, lo = split(mat_times(tr_v[24 + i], paths[i // 2]))
-        for j, part in enumerate((hi, lo, hi)):
-            g_v[(4 * j + i) * RANK : (4 * j + i + 1) * RANK, :] = part
-    raise_level(16, 8)
-    highs = [uhi[24 + i] for i in range(4)]
-    p_v[...] = nn(beside(*highs, *highs, *[ulo[24 + i] for i in range(4)]), g_v[...])
-
-    pl.semaphore_wait(barrier, len(peers))
-    mine_rows = pl.ds(pl.multiple_of(core * HALF, HALF), HALF)
-    other_rows = pl.ds(pl.multiple_of((1 - core) * HALF, HALF), HALF)
-
-    def remote(src, dst, send, recv, peer):
-        return pltpu.make_async_remote_copy(
-            src_ref=src, dst_ref=dst, send_sem=send, recv_sem=recv, device_id=peer, device_id_type=MESH
-        )
-
-    swap = remote(p_v.at[other_rows], pp_v, cs_s.at[0], cs_r.at[0], partner)
-    swap.start()
     swap.wait_recv()
     zbuf[z] = (p_v[mine_rows] + pp_v[...]).astype(BF)
     zsends = [remote(zbuf.at[z], zbuf.at[z], zs.at[k], zr.at[k], zpeers[k]) for k in range(NZ - 1)]
@@ -292,25 +292,27 @@
 
 def finish(near, bs_v, d0_v, h_v, ups, out, sum_v, sem):
     u8s = beside(ups[...], ups[...])
-
-    def top(i):
-        return nn(u8s, h_v[:, 2 * i * RANK : 2 * (i + 1) * RANK])
-
-    copies = []
-    ahead = top(0)
-    for i in range(LEAVES // 2):
-        part = ahead
-        if i + 1 < LEAVES // 2:
-            ahead = top(i + 1)
-        for j in range(2):
-            leaf = 2 * i + j
+    pairs = LEAVES // 2
+    tops, downs, copies = {}, {}, []
+
+    def final(i):
+        for leaf in (2 * i, 2 * i + 1):
             where = pl.ds(leaf * LEAF, LEAF)
             own = bs_v[leaf]
-            down = split(d0_v[leaf] + part[:, j * RANK : (j + 1) * RANK])
-            sum_v[where] = near[where] + nt(beside(own, own), beside(*down))
+            sum_v[where] = near[where] + nt(beside(own, own), beside(*downs[leaf]))
         where = pl.ds(2 * i * LEAF, 2 * LEAF)
         copies.append(pltpu.make_async_copy(sum_v.at[where], out.at[where], sem.at[i]))
         copies[-1].start()
+
+    for step in range(pairs + 2):
+        if step < pairs:
+            tops[step] = nn(u8s, h_v[:, 2 * step * RANK : 2 * (step + 1) * RANK])
+        if 1 <= step <= pairs:
+            for j in range(2):
+                leaf = 2 * (step - 1) + j
+                downs[leaf] = split(d0_v[leaf] + tops[step - 1][:, j * RANK : (j + 1) * RANK])
+        if step >= 2:
+            final(step - 2)
     for cp in copies:
         cp.wait()
 

time: 23 us -> 22.7 us (0.987)
  Pallas kernels: 22.8 us -> 22.5 us
    pallas_call x1, Pallas kernels: 2.31 us -> 2.02 us  [local(): pl.pallas_call(finish, out_shape=jax.ShapeDtypeStruct((rows, COLS), F32),...]
where the time goes in v6:
time: 22.7 us; the launch traced here: 22.5 us
  Pallas kernels  22.5 us (99%)
    pallas_call x1, Pallas kernels, local(): pl.pallas_call(kernel, out_shape=(vm((rows, COLS), F32), vm((LEAVES, LEAF...  20.5 us
    pallas_call x1, Pallas kernels, local(): pl.pallas_call(finish, out_shape=jax.ShapeDtypeStruct((rows, COLS), F32),...  2.02 us

profile of v6, /device:TPU:1, one launch (start us, length us, event | category | flops | bytes accessed | tf_op | source)
XLA Modules:
  0.0 22.5 jit_solution(500262491419283516)
XLA Ops:
  0.0 20.5 %shard_map.82 = (f32[4096,128]{1,0:T(8,128)S(1)}, bf16[16,256,128]{2,1,0:T(8,128)(2,1)S(1)}, f32[16,128,128]{2,1,0:T(8,128)S(1)}, bf16[768,2048]{1,0:T(8,128)(2,1)S(1)}, bf16[128,384]{1,0:T(8,128)(2,1)S(1)}) custom-call(f32[8,4096]{1,0:T(8,128)} %points.1, bf16[4096,128]{1,0:T(8,128)(2,1)} %charges.1, s32[4096]{0:T(1024)} %order.1, ...), custom_call_target="tpu_custom_call" | custom-call | tf_op jit(solution)/shard_map/pallas_call | solution.py:325
  20.5 2.0 %shard_map.83 = f32[4096,128]{1,0:T(8,128)} custom-call(f32[4096,128]{1,0:T(8,128)S(1)} %get-tuple-element.10.near, bf16[16,256,128]{2,1,0:T(8,128)(2,1)S(1)} %get-tuple-element.11.bs_v, f32[16,128,128]{2,1,0:T(8,128)S(1)} %get-tuple-element.12.d0_v, bf16[768,2048]{1,0:T(8,128)(2,1)S(1)} %get-tuple-element.13.h_v, bf16[128,384]{1,0:T(8,128)(2,1)S(1)} %get-tuple-element.14.ups), custom_call_target="tpu_custom_call" | custom-call | tf_op jit(solution)/shard_map/pallas_call | solution.py:382

commit v7 on v6

--- a/solution.py
+++ b/solution.py
@@ -80,14 +80,16 @@
         cp.start()
         return cp
 
+    barrier = pltpu.get_barrier_semaphore()
+    peers = [zpeers[k] for k in (3, 2, 4, 1, 5)] + xpeers + [zpeers[0], zpeers[6], partner]
+    for peer in peers[:5]:
+        pl.semaphore_signal(barrier, inc=1, device_id=peer, device_id_type=MESH)
+
     order_cp = load(order, ord_v, 0)
     charges_cp = load(charges, q_v, 1)
     basis_cp = load(basis, bas_v, 2)
     trans_cp = load(trans, tr_v, 3)
-
-    barrier = pltpu.get_barrier_semaphore()
-    peers = [zpeers[k] for k in (3, 2, 4, 1, 5)] + xpeers + [zpeers[0], zpeers[6], partner]
-    for peer in peers:
+    for peer in peers[5:]:
         pl.semaphore_signal(barrier, inc=1, device_id=peer, device_id_type=MESH)
 
     def span(leaf):
@@ -127,11 +129,10 @@
     raise_level(0, 16)
     for i in range(4):
         hi, lo = split(mat_times(tr_v[24 + i], paths[i // 2]))
-        for j, part in enumerate((hi, lo, hi)):
-            g_v[(4 * j + i) * RANK : (4 * j + i + 1) * RANK, :] = part
+        g_v[i * RANK : (i + 1) * RANK, :] = beside(hi, lo)
     raise_level(16, 8)
-    highs = [uhi[24 + i] for i in range(4)]
-    p_v[...] = nn(beside(*highs, *highs, *[ulo[24 + i] for i in range(4)]), g_v[...])
+    both = nn(beside(*[uhi[24 + i] for i in range(4)]), g_v[...])
+    p_v[...] = both[:, :RANK] + both[:, RANK:] + nn(beside(*[ulo[24 + i] for i in range(4)]), g_v[:, :RANK])
 
     pl.semaphore_wait(barrier, len(peers))
     mine_rows = pl.ds(pl.multiple_of(core * HALF, HALF), HALF)
@@ -161,7 +162,7 @@
     swap.wait_recv()
     zbuf[z] = (p_v[mine_rows] + pp_v[...]).astype(BF)
     zsends = [remote(zbuf.at[z], zbuf.at[z], zs.at[k], zr.at[k], zpeers[k]) for k in range(NZ - 1)]
-    for k in (3, 2, 4, 1, 5, 0, 6):
+    for k in (3, 4, 2, 5, 1, 6, 0):
         zsends[k].start()
 
     raise_level(24, 4)
@@ -282,12 +283,11 @@
     for i in range(LEAVES):
         d0_v[i] = side_v[i] + times_t(down[i // 2], tr_v[i])
 
+    for cp in [swap, swap4, back] + zsends + xsends:
+        cp.wait_send()
     for cp in xsends:
         cp.wait_recv()
     ups[...] = beside(xbuf[sibling(x)], xbuf[far], xbuf[far + 1])
-
-    for cp in [swap, swap4] + zsends + xsends + [back]:
-        cp.wait_send()
 
 
 def finish(near, bs_v, d0_v, h_v, ups, out, sum_v, sem):
@@ -359,7 +359,7 @@
             vm((NZ, HALF, RANK), BF),
             vm((NX, COLS, RANK), BF),
             vm((COLS, RANK), F32),
-            vm((12 * RANK, RANK), BF),
+            vm((4 * RANK, 2 * RANK), BF),
             vm((NZ * RANK, 2 * RANK), BF),
             vm((LEAVES * RANK, 3 * RANK), BF),
             vm((3 * RANK, 3 * RANK), BF),

time: 22.7 us -> 22.6 us (level)
  no operation moved by 1% of the time
where the time goes in v7:
time: 22.6 us; the launch traced here: 22.4 us
  Pallas kernels  22.4 us (99%)
    pallas_call x1, Pallas kernels, local(): pl.pallas_call(kernel, out_shape=(vm((rows, COLS), F32), vm((LEAVES, LEAF...  20.4 us
    pallas_call x1, Pallas kernels, local(): pl.pallas_call(finish, out_shape=jax.ShapeDtypeStruct((rows, COLS), F32),...  2.02 us

profile of v7, /device:TPU:1, one launch (start us, length us, event | category | flops | bytes accessed | tf_op | source)
XLA Modules:
  0.0 22.4 jit_solution(6737289409862752391)
XLA Ops:
  0.0 20.4 %shard_map.82 = (f32[4096,128]{1,0:T(8,128)S(1)}, bf16[16,256,128]{2,1,0:T(8,128)(2,1)S(1)}, f32[16,128,128]{2,1,0:T(8,128)S(1)}, bf16[768,2048]{1,0:T(8,128)(2,1)S(1)}, bf16[128,384]{1,0:T(8,128)(2,1)S(1)}) custom-call(f32[8,4096]{1,0:T(8,128)} %points.1, bf16[4096,128]{1,0:T(8,128)(2,1)} %charges.1, s32[4096]{0:T(1024)} %order.1, ...), custom_call_target="tpu_custom_call" | custom-call | tf_op jit(solution)/shard_map/pallas_call | solution.py:325
  20.4 2.0 %shard_map.83 = f32[4096,128]{1,0:T(8,128)} custom-call(f32[4096,128]{1,0:T(8,128)S(1)} %get-tuple-element.10.near, bf16[16,256,128]{2,1,0:T(8,128)(2,1)S(1)} %get-tuple-element.11.bs_v, f32[16,128,128]{2,1,0:T(8,128)S(1)} %get-tuple-element.12.d0_v, bf16[768,2048]{1,0:T(8,128)(2,1)S(1)} %get-tuple-element.13.h_v, bf16[128,384]{1,0:T(8,128)(2,1)S(1)} %get-tuple-element.14.ups), custom_call_target="tpu_custom_call" | custom-call | tf_op jit(solution)/shard_map/pallas_call | solution.py:382

commit v8 on v7

--- a/solution.py
+++ b/solution.py
@@ -145,6 +145,12 @@
 
     swap = remote(p_v.at[other_rows], pp_v, cs_s.at[0], cs_r.at[0], partner)
     swap.start()
+    swap.wait_recv()
+    zbuf[z] = (p_v[mine_rows] + pp_v[...]).astype(BF)
+    zsends = [remote(zbuf.at[z], zbuf.at[z], zs.at[k], zr.at[k], zpeers[k]) for k in range(NZ - 1)]
+    for k in (3, 4, 2, 5, 1, 6, 0):
+        zsends[k].start()
+
     late = [
         load(points, pts_v, 4),
         load(top_t.at[pl.ds(x * 8, 8)], t5_v, 5),
@@ -159,16 +165,10 @@
         load(top_c.at[62], c_v.at[5], 14),
         load(coup, cp_v, 15),
     ]
-    swap.wait_recv()
-    zbuf[z] = (p_v[mine_rows] + pp_v[...]).astype(BF)
-    zsends = [remote(zbuf.at[z], zbuf.at[z], zs.at[k], zr.at[k], zpeers[k]) for k in range(NZ - 1)]
-    for k in (3, 4, 2, 5, 1, 6, 0):
-        zsends[k].start()
 
     raise_level(24, 4)
     u4_v[...] = parent(read(28), read(29), tr_v[28:30])
     swap4 = remote(u4_v, u4p_v, cs_s.at[1], cs_r.at[1], partner)
-    swap4.start()
     for cp in late:
         cp.wait()
 
@@ -234,6 +234,7 @@
         beside(across[0][0], across[0][0], across[0][1]),
         beside(across[1][0], across[1][0], across[1][1]),
     )
+    swap4.start()
     for leaf in range(LEAVES):
         bs_v[leaf] = nn(pick_v[leaf], bas_v[leaf]).astype(BF)
     for pair in range(15):

time: 22.6 us -> 22.6 us (level)
  no operation moved by 1% of the time
where the time goes in v8:
time: 22.6 us; the launch traced here: 22.4 us
  Pallas kernels  22.4 us (99%)
    pallas_call x1, Pallas kernels, local(): pl.pallas_call(kernel, out_shape=(vm((rows, COLS), F32), vm((LEAVES, LEAF...  20.4 us
    pallas_call x1, Pallas kernels, local(): pl.pallas_call(finish, out_shape=jax.ShapeDtypeStruct((rows, COLS), F32),...  2.02 us

profile of v8, /device:TPU:1, one launch (start us, length us, event | category | flops | bytes accessed | tf_op | source)
XLA Modules:
  0.0 22.4 jit_solution(8041664909978631379)
XLA Ops:
  0.0 20.4 %shard_map.82 = (f32[4096,128]{1,0:T(8,128)S(1)}, bf16[16,256,128]{2,1,0:T(8,128)(2,1)S(1)}, f32[16,128,128]{2,1,0:T(8,128)S(1)}, bf16[768,2048]{1,0:T(8,128)(2,1)S(1)}, bf16[128,384]{1,0:T(8,128)(2,1)S(1)}) custom-call(f32[8,4096]{1,0:T(8,128)} %points.1, bf16[4096,128]{1,0:T(8,128)(2,1)} %charges.1, s32[4096]{0:T(1024)} %order.1, ...), custom_call_target="tpu_custom_call" | custom-call | tf_op jit(solution)/shard_map/pallas_call | solution.py:326
  20.4 2.0 %shard_map.83 = f32[4096,128]{1,0:T(8,128)} custom-call(f32[4096,128]{1,0:T(8,128)S(1)} %get-tuple-element.10.near, bf16[16,256,128]{2,1,0:T(8,128)(2,1)S(1)} %get-tuple-element.11.bs_v, f32[16,128,128]{2,1,0:T(8,128)S(1)} %get-tuple-element.12.d0_v, bf16[768,2048]{1,0:T(8,128)(2,1)S(1)} %get-tuple-element.13.h_v, bf16[128,384]{1,0:T(8,128)(2,1)S(1)} %get-tuple-element.14.ups), custom_call_target="tpu_custom_call" | custom-call | tf_op jit(solution)/shard_map/pallas_call | solution.py:383

commit v9 on v8

--- a/solution.py
+++ b/solution.py
@@ -56,7 +56,7 @@
 
 
 def kernel(
-    points, charges, order, basis, trans, coup, top_t, top_c, near, bs_v, d0_v, h_v, ups,
+    points, charges, order, basis, trans, coup, top_t, top_c, near, bs_v, h_v, ups,
     pts_v, q_v, ord_v, bas_v, tr_v, cp_v, t5_v, t6_v, t7_v, t8_v, c_v,
     uhi, ulo, side_v, lhs_v, rhs_v, e_v, pick_v,
     p_v, pp_v, u4_v, u4p_v, zbuf, xbuf, d5_v, g_v, q2_v, e0_v, src_v, m_v, qp_v,
@@ -282,7 +282,9 @@
     for start, count in ((28, 2), (24, 4), (16, 8)):
         down = [split(side_v[start + i] + times_t(down[i // 2], tr_v[start + i])) for i in range(count)]
     for i in range(LEAVES):
-        d0_v[i] = side_v[i] + times_t(down[i // 2], tr_v[i])
+        uhi[i], ulo[i] = split(side_v[i] + times_t(down[i // 2], tr_v[i]))
+    for i in range(LEAVES):
+        near[span(i), :] += nt(beside(bs_v[i], bs_v[i]), beside(uhi[i], ulo[i]))
 
     for cp in [swap, swap4, back] + zsends + xsends:
         cp.wait_send()
@@ -291,7 +293,7 @@
     ups[...] = beside(xbuf[sibling(x)], xbuf[far], xbuf[far + 1])
 
 
-def finish(near, bs_v, d0_v, h_v, ups, out, sum_v, sem):
+def finish(near, bs_v, h_v, ups, out, sum_v, sem):
     u8s = beside(ups[...], ups[...])
     pairs = LEAVES // 2
     tops, downs, copies = {}, {}, []
@@ -311,7 +313,7 @@
         if 1 <= step <= pairs:
             for j in range(2):
                 leaf = 2 * (step - 1) + j
-                downs[leaf] = split(d0_v[leaf] + tops[step - 1][:, j * RANK : (j + 1) * RANK])
+                downs[leaf] = split(tops[step - 1][:, j * RANK : (j + 1) * RANK])
         if step >= 2:
             final(step - 2)
     for cp in copies:
@@ -328,12 +330,11 @@
         out_shape=(
             vm((rows, COLS), F32),
             vm((LEAVES, LEAF, RANK), BF),
-            vm((LEAVES, COLS, RANK), F32),
             vm((6 * RANK, LEAVES * RANK), BF),
             vm((COLS, 3 * RANK), BF),
         ),
         in_specs=[pl.BlockSpec(memory_space=pltpu.HBM)] * 8,
-        out_specs=[pl.BlockSpec(memory_space=vm)] * 5,
+        out_specs=[pl.BlockSpec(memory_space=vm)] * 4,
         scratch_shapes=[
             vm((8, rows), F32),
             vm((rows, COLS), BF),
@@ -383,7 +384,7 @@
     return pl.pallas_call(
         finish,
         out_shape=jax.ShapeDtypeStruct((rows, COLS), F32),
-        in_specs=[pl.BlockSpec(memory_space=vm)] * 5,
+        in_specs=[pl.BlockSpec(memory_space=vm)] * 4,
         out_specs=pl.BlockSpec(memory_space=pltpu.HBM),
         scratch_shapes=[vm((rows, COLS), F32), dma((LEAVES // 2,))],
         compiler_params=pltpu.CompilerParams(vmem_limit_bytes=16 * 1024 * 1024),

time: 22.6 us -> 22.6 us (level)
  no operation moved by 1% of the time
where the time goes in v9:
time: 22.6 us; the launch traced here: 22.4 us
  Pallas kernels  22.4 us (99%)
    pallas_call x1, Pallas kernels, local(): pl.pallas_call(kernel, out_shape=(vm((rows, COLS), F32), vm((LEAVES, LEAF...  20.4 us
    pallas_call x1, Pallas kernels, local(): pl.pallas_call(finish, out_shape=jax.ShapeDtypeStruct((rows, COLS), F32),...  2.03 us

profile of v9, /device:TPU:1, one launch (start us, length us, event | category | flops | bytes accessed | tf_op | source)
XLA Modules:
  0.0 22.4 jit_solution(11177895035176290656)
XLA Ops:
  0.0 20.4 %shard_map.82 = (f32[4096,128]{1,0:T(8,128)S(1)}, bf16[16,256,128]{2,1,0:T(8,128)(2,1)S(1)}, bf16[768,2048]{1,0:T(8,128)(2,1)S(1)}, bf16[128,384]{1,0:T(8,128)(2,1)S(1)}) custom-call(f32[8,4096]{1,0:T(8,128)} %points.1, bf16[4096,128]{1,0:T(8,128)(2,1)} %charges.1, s32[4096]{0:T(1024)} %order.1, bf16[16,256,128]{2,1,0:T(8,128)(2,1)} %basis.1, ...), custom_call_target="tpu_custom_call" | custom-call | tf_op jit(solution)/shard_map/pallas_call | solution.py:328
  20.4 2.0 %shard_map.83 = f32[4096,128]{1,0:T(8,128)} custom-call(f32[4096,128]{1,0:T(8,128)S(1)} %get-tuple-element.9.near, bf16[16,256,128]{2,1,0:T(8,128)(2,1)S(1)} %get-tuple-element.10.bs_v, bf16[768,2048]{1,0:T(8,128)(2,1)S(1)} %get-tuple-element.11.h_v, bf16[128,384]{1,0:T(8,128)(2,1)S(1)} %get-tuple-element.12.ups), custom_call_target="tpu_custom_call" | custom-call | tf_op jit(solution)/shard_map/pallas_call | solution.py:384
